TPU v7x, 128 devices: a whole 4x4x4 slice. The times are simulated.
128 devices in a mesh: grp: 8 (over z, core), blk: 16 (over x, y).
Axes of the slice: x: 4, y: 4, z: 4, core: 2. Of those that a mesh axis runs over, the one named last changes fastest.
Arguments:
- left_tensor: bfloat16 [8, 3072, 768], P('grp', 'blk'), may hold values from -6 to 6
- right_tensor: bfloat16 [8, 768, 3072], P('grp', 'blk'), may hold values from -0.21875 to 0.21875
- diag_gate: float32 [8, 3072], P('grp'), may hold values from 0.2 to 1
- hop_gate: float32 [8, 3072], P('grp'), may hold values from -0.6 to 0.6
- sketch: bfloat16 [3072, 768], replicated, may hold values from -0.109375 to 0.109375
- sector_rows: int32 [8], P('grp'), may hold values from 1536 to 3072, as said below
- kept: int32 [8], P('grp'), may hold values from 384 to 768, as said below
Outputs:
- left_out: float32 [8, 3072, 768], P('grp', 'blk')
- right_out: float32 [3072, 8, 768], P('blk', 'grp')
Inputs may be any that keep to these rules, and one draw needn't show every extreme that they name: `sector_rows`: reached by some sector in every draw, at both ends. `kept`: reached by some sector in every draw, at both ends.
All inputs are finite; a program needn't handle non-finite values.
Results may differ from a plain program's by a relative error of at most 0.022.
Values may be sent and summed in bfloat16 or wider, within the bound.
A program may use at most 128 MiB of HBM per device.

v0:
```python
import math

import jax
import jax.numpy as jnp
from jax import lax
from jax.sharding import PartitionSpec as P


def padded_2(x, sides, width):
    for axis, dim in sides:
        size, length = (lax.axis_size(axis), x.shape[dim])
        up = [(i, (i + 1) % size) for i in range(size - 1)]
        down = [(j, i) for i, j in up]
        last = lax.slice_in_dim(x, length - width, length, axis=dim)
        initial = lax.slice_in_dim(x, 0, width, axis=dim)
        before = lax.ppermute(last, axis, up)
        after = lax.ppermute(initial, axis, down)
        x = jnp.concatenate([before, x, after], axis=dim)
    return x


def body(left_tensor, right_tensor, diag_gate, hop_gate, sketch, sector_rows, kept):
    sectors_here, rows_here, middle_states = left_tensor.shape
    kept_width = sketch.shape[1]
    blk_count = lax.axis_size("blk")
    total_rows = rows_here * blk_count
    theta_full = jnp.einsum(
        "srx,sxc->src",
        left_tensor,
        lax.all_gather(right_tensor, "blk", axis=1, tiled=True),
        preferred_element_type=jnp.float32,
    ).astype(jnp.bfloat16)
    padded = padded_2(theta_full, (("grp", 0),), 1).astype(jnp.float32)
    centre = padded[1:-1]
    mixed_wide = diag_gate[:, None, :] * centre + hop_gate[:, None, :] * (padded[:-2] + padded[2:])
    row_index = lax.axis_index("blk") * rows_here + jnp.arange(rows_here, dtype=jnp.int32)
    row_live = (row_index[None, :] < sector_rows[:, None]).astype(jnp.float32)
    mixed_b = (mixed_wide * row_live[:, :, None]).astype(jnp.bfloat16)
    col_live = (jnp.arange(kept_width, dtype=jnp.int32)[None, :] < kept[:, None]).astype(
        jnp.float32
    )
    sketched = jnp.einsum("src,ck->srk", mixed_b, sketch, preferred_element_type=jnp.float32)
    sketched = (sketched * col_live[:, None, :]).astype(jnp.bfloat16)
    gram_local = jnp.einsum("srk,srj->skj", sketched, sketched, preferred_element_type=jnp.float32)
    gram_mat = lax.psum(gram_local, "blk")
    gram_mat = (
        gram_mat + (1.0 - col_live)[:, :, None] * jnp.eye(kept_width, dtype=jnp.float32)[None]
    )
    factor = jnp.linalg.cholesky(gram_mat)
    sketch_wide = sketched.astype(jnp.float32)
    ortho_basis = lax.linalg.triangular_solve(
        factor, sketch_wide, left_side=False, lower=True, transpose_a=True
    )
    row_scale = math.sqrt(total_rows)
    left_out = ortho_basis * row_scale
    basis_b = ortho_basis.astype(jnp.bfloat16)
    summed = lax.psum_scatter(
        jnp.einsum("src,srk->csk", mixed_b, basis_b, preferred_element_type=jnp.float32).astype(
            jnp.bfloat16
        ),
        "blk",
        scatter_dimension=0,
        tiled=True,
    ).astype(jnp.float32)
    right_out = summed / row_scale
    return (left_out, right_out)


def solution(mesh):
    in_specs = (
        P("grp", "blk", None),
        P("grp", "blk", None),
        P("grp", None),
        P("grp", None),
        P(),
        P("grp"),
        P("grp"),
    )
    out_specs = (P("grp", "blk", None), P("blk", "grp", None))
    return jax.shard_map(body, mesh=mesh, in_specs=in_specs, out_specs=out_specs, check_vma=False)
```

profile of v0, /device:TPU:0, one launch (start us, length us, event | category | flops | bytes accessed | tf_op | source)
XLA Modules:
  0.0 565.9 jit_solution(544307361954773672)
XLA Ops:
  8.0 58.6 %all-gather.2.cloned.1.call-done = bf16[1,768,3072]{2,1,0:T(8,128)(2,1)} async-done(((bf16[1,48,3072]{2,1,0:T(8,128)(2,1)}), bf16[1,768,3072]{2,1,0:T(8,128)(2,1)}) %all-gather.2.cloned.1.call-update) | async-done | bytes 4718608 | tf_op jit(solution)/shard_map/all_gather | solution.py:30
  66.6 3.5 fusion.6
  70.1 1.8 collective-permute-start
  74.6 3.5 collective-permute-done.1
  78.0 1.8 maximum_convert_fusion
  81.9 1.9 convolution_bitcast_fusion
  84.4 103.3 %all-reduce.3.cloned.1.call-done = f32[1,768,768]{1,2,0:T(8,128)} async-done(((f32[1,768,768]{1,2,0:T(8,128)}), f32[1,768,768]{1,2,0:T(8,128)}) %all-reduce.3.cloned.1.call-update) | async-done | bytes 2359312 | tf_op jit(solution)/shard_map/psum | solution.py:45
  187.7 3.2 select_add_fusion
  190.9 2.2 copy.25
  193.1 2.0 fusion.13
  196.5 11.7 %custom-call.52 = f32[1,128,128]{2,1,0:T(8,128)S(1)} custom-call(f32[1,128,128]{2,1,0:T(8,128)S(1)} %cholesky.424), custom_call_target="Cholesky" | custom-call | tf_op jit(solution)/shard_map/jit(cholesky)/cholesky | solution.py:49
  208.2 9.8 %custom-call.53 = f32[1,1,128,128]{2,3,1,0:T(8,128)S(1)} custom-call(f32[1,1,128,128]{3,2,1,0:T(8,128)S(1)} %get-tuple-element.51), custom_call_target="InvertDiagBlocksLowerTriangular" | custom-call | tf_op jit(solution)/shard_map/jit(cholesky)/cholesky | solution.py:49
  219.6 1.5 fusion.16
  221.2 11.7 %custom-call.54 = f32[1,128,128]{2,1,0:T(8,128)S(1)} custom-call(f32[1,128,128]{2,1,0:T(8,128)S(1)} %cholesky.428), custom_call_target="Cholesky" | custom-call | tf_op jit(solution)/shard_map/jit(cholesky)/cholesky | solution.py:49
  236.0 11.5 %custom-call.55 = f32[1,1,128,128]{2,3,1,0:T(8,128)} custom-call(f32[1,1,128,128]{3,2,1,0:T(8,128)} %get-tuple-element.49), custom_call_target="InvertDiagBlocksLowerTriangular" | custom-call | tf_op jit(solution)/shard_map/jit(cholesky)/cholesky | solution.py:49
  249.7 1.9 fusion.18
  253.0 13.2 %custom-call.56 = f32[1,128,128]{2,1,0:T(8,128)} custom-call(f32[1,128,128]{2,1,0:T(8,128)} %cholesky.433), custom_call_target="Cholesky" | custom-call | tf_op jit(solution)/shard_map/jit(cholesky)/cholesky | solution.py:49
  266.2 1.5 select_reduce_fusion.3
  267.7 1.6 copy.30
  270.1 11.3 %custom-call.57 = f32[1,1,128,128]{2,3,1,0:T(8,128)} custom-call(f32[1,1,128,128]{3,2,1,0:T(8,128)} %get-tuple-element.47), custom_call_target="InvertDiagBlocksLowerTriangular" | custom-call | tf_op jit(solution)/shard_map/jit(cholesky)/cholesky | solution.py:49
  282.7 2.1 fusion.20
  286.1 13.6 %custom-call.58 = f32[1,128,128]{2,1,0:T(8,128)} custom-call(f32[1,128,128]{2,1,0:T(8,128)} %cholesky.438), custom_call_target="Cholesky" | custom-call | tf_op jit(solution)/shard_map/jit(cholesky)/cholesky | solution.py:49
  299.6 1.5 select_reduce_fusion.2
  301.1 1.6 copy.32
  303.5 11.3 %custom-call.59 = f32[1,1,128,128]{2,3,1,0:T(8,128)} custom-call(f32[1,1,128,128]{3,2,1,0:T(8,128)} %get-tuple-element.45), custom_call_target="InvertDiagBlocksLowerTriangular" | custom-call | tf_op jit(solution)/shard_map/jit(cholesky)/cholesky | solution.py:49
  316.0 1.9 fusion.22
  319.2 13.2 %custom-call.60 = f32[1,128,128]{2,1,0:T(8,128)} custom-call(f32[1,128,128]{2,1,0:T(8,128)} %cholesky.443), custom_call_target="Cholesky" | custom-call | tf_op jit(solution)/shard_map/jit(cholesky)/cholesky | solution.py:49
  332.4 2.0 select_reduce_fusion.1
  334.4 1.6 copy.34
  336.8 11.3 %custom-call.61 = f32[1,1,128,128]{2,3,1,0:T(8,128)} custom-call(f32[1,1,128,128]{3,2,1,0:T(8,128)} %get-tuple-element.43), custom_call_target="InvertDiagBlocksLowerTriangular" | custom-call | tf_op jit(solution)/shard_map/jit(cholesky)/cholesky | solution.py:49
  349.2 2.3 fusion.34
  351.5 13.2 %custom-call.62 = f32[1,128,128]{2,1,0:T(8,128)} custom-call(f32[1,128,128]{2,1,0:T(8,128)} %fusion.34), custom_call_target="Cholesky" | custom-call | tf_op jit(solution)/shard_map/jit(cholesky)/cholesky | solution.py:49
  366.1 1.6 copy.36
  376.9 1.6 select_select_fusion
  378.5 22.4 %while.1 = (s32[]{:T(128)}, f32[1,768,768]{1,2,0:T(8,128)}, s32[6,2]{0,1:T(2,128)S(1)}, f32[6,1,128,128]{3,2,1,0:T(8,128)}, s32[]{:T(128)}) while((s32[]{:T(128)}, f32[1,768,768]{1,2,0:T(8,128)}, s32[6,2]{0,1:T(2,128)S(1)}, f32[6,1,128,128]{3,2,1,0:T(8,128)}, s32[]{:T(128)}) %tuple.47), condition=%wide.while_cond, body=%wide.while_body.sunk | while | flops 2 | bytes 393833 | solution.py:51
  379.2 2.3 constant_dynamic-slice_fusion.5
  382.9 2.3 constant_dynamic-slice_fusion.5
  386.7 2.3 constant_dynamic-slice_fusion.5
  390.4 2.3 constant_dynamic-slice_fusion.5
  394.1 2.3 constant_dynamic-slice_fusion.5
  397.9 2.3 constant_dynamic-slice_fusion.5
  400.9 59.8 %custom-call.63 = f32[1,6,128,128]{2,3,1,0:T(8,128)S(1)} custom-call(f32[1,6,128,128]{3,2,1,0:T(8,128)} %bitcast.298), custom_call_target="InvertDiagBlocksLowerTriangular" | custom-call | tf_op jit(solution)/shard_map/triangular_solve | solution.py:51
  463.7 1.4 fusion.26
  465.4 1.4 fusion.28
  467.1 1.5 fusion.30
  468.9 3.6 fusion.2
  472.5 6.6 %copy.46 = bf16[3072,768]{1,0:T(8,128)(2,1)} copy(bf16[3072,768]{0,1:T(8,128)(2,1)} %fusion.2) | data formatting | bytes 9437184
  480.0 76.8 %reduce-scatter.4.cloned.1.call-done = bf16[192,768]{1,0:T(8,128)(2,1)} async-done(((bf16[3072,768]{1,0:T(8,128)(2,1)}), bf16[192,768]{1,0:T(8,128)(2,1)}) %reduce-scatter.4.cloned.1.call-update) | async-done | bytes 294928
  (117 shorter events, 45.3 us)
Async XLA Ops:
  7.2 59.4 %copy-start = (bf16[1,192,768]{2,1,0:T(8,128)(2,1)S(1)}, bf16[1,192,768]{2,1,0:T(8,128)(2,1)}, u32[]{:S(2)}) copy-start(bf16[1,192,768]{2,1,0:T(8,128)(2,1)} %param.7) | copy-start | bytes 884740
  7.2 59.4 %all-gather.2.cloned.1.call-start = ((), (), s32[]{:S(2)}) async-start(), calls=%async_computation.1 | async-start | bytes 5013504 | tf_op jit(solution)/shard_map/all_gather | solution.py:30
  7.9 179.7 %all-reduce.3.cloned.1.call-start = ((), (), s32[]{:S(2)}) async-start(), calls=%async_computation.2 | async-start | bytes 4718592 | tf_op jit(solution)/shard_map/psum | solution.py:45
  66.6 14.1 %slice-start = ((s8[4718592]{0:T(1024)(128)(4,1)}), s8[524288]{0:T(1024)(128)(4,1)S(1)}, s32[]{:S(2)}) async-start(s8[4718592]{0:T(1024)(128)(4,1)} %bitcast.283), calls=%async_computation.4 | async-start | bytes 1048576
  70.1 4.5 collective-permute-start
  71.9 6.1 %collective-permute-start.1 = (bf16[1,192,3072]{2,1,0:T(8,128)(2,1)S(1)}, bf16[1,192,3072]{2,1,0:T(8,128)(2,1)}, u32[]{:S(2)}, u32[]{:S(2)}) collective-permute-start(bf16[1,192,3072]{2,1,0:T(8,128)(2,1)S(1)} %fusion.6), channel_id=1, source_target_pairs={{16,0},{32,16},{48,32},{64,48},{80,64},{96,80},{112,96},{17,1},{33... | collective-permute-start | bytes 3538952 | tf_op jit(solution)/shard_map/ppermute | solution.py:17
  74.5 5.3 copy-start.10
  74.5 5.3 copy-start.11
  74.5 6.2 %slice-start.1 = ((s8[4718592]{0:T(1024)(128)(4,1)}), s8[4194304]{0:T(1024)(128)(4,1)S(1)}, s32[]{:S(2)}) async-start(s8[4718592]{0:T(1024)(128)(4,1)} %bitcast.283), calls=%async_computation.5 | async-start | bytes 8388608
  80.7 1.1 copy-start.1
  83.8 473.0 %reduce-scatter.4.cloned.1.call-start = ((), (), s32[]{:S(2)}) async-start(), calls=%async_computation.3 | async-start | bytes 5013504
  195.1 1.4 copy-start.3
  219.6 14.6 %copy-start.4 = (f32[640,128]{0,1:T(8,128)}, f32[640,128]{0,1:T(8,128)S(1)}, u32[]{:S(2)}) copy-start(f32[640,128]{0,1:T(8,128)S(1)} %copy.26) | copy-start | bytes 983044
  221.1 13.1 %copy-start.6 = (f32[1,640,128]{2,1,0:T(8,128)}, f32[1,640,128]{2,1,0:T(8,128)S(1)}, u32[]{:S(2)}) copy-start(f32[1,640,128]{2,1,0:T(8,128)S(1)} %fusion.16) | copy-start | bytes 983044
  235.0 1.0 copy-start.5
  251.7 0.7 copy-start.7
  284.8 0.7 copy-start.8
  317.9 0.7 copy-start.9
  376.9 1.6 copy-start.12
  463.5 5.5 copy-start.2
Sparse Core Ops, SparseCore 0:
  10.2 56.3 all-gather.1
  83.9 103.6 all-reduce.2
  479.3 77.5 reduce-scatter.3
where the time goes:
time: 572 us; the launch traced here: 566 us
  waiting for transfers between devices  243 us (42%)
  other arithmetic  214 us (37%)
  local copies, waits for them, and re-layouts  51.9 us (9%)
  matrix products  34.4 us (6%)
  between operations  19.5 us (3%)
    another operation x22, other arithmetic, body(): factor = jnp.linalg.cholesky(gram_mat)  143 us
    psum x1, waiting for transfers between devices, body(): gram_mat = lax.psum(gram_local, 'blk')  103 us
    unnamed x4, waiting for transfers between devices  77.5 us
    another operation x3, other arithmetic, body(): lax.linalg.triangular_solve(factor, sketch_wide, left_side=False, lower=T...  61.9 us
    all_gather x1, waiting for transfers between devices, body(): lax.all_gather(right_tensor, 'blk', axis=1, tiled=True)  58.6 us
    another operation x30, local copies, waits for them, and re-layouts  22.3 us
    another operation x10, matrix products, body(): factor = jnp.linalg.cholesky(gram_mat)  16.2 us
    another operation x19, local copies, waits for them, and re-layouts, body(): factor = jnp.linalg.cholesky(gram_mat)  15 us
  transfers between devices with their start and end apart: 5, of which 4 were waited for; matrix products, arithmetic and copies ran while one was open for 0% of the time, Pallas kernels for 0%

commit v1 on v0

v1 whole, which is shorter than its diff:
```python
import math

import jax
import jax.numpy as jnp
from jax import lax
from jax.experimental import pallas as pl
from jax.experimental.pallas import tpu as pltpu
from jax.sharding import PartitionSpec as P

HIGH = lax.Precision.HIGHEST
B = 128


def reciprocal(p):
    r = pl.reciprocal(p, approx=True)
    return r * (2.0 - p * r)


def pivot_inverse(a):
    lane = lax.broadcasted_iota(jnp.int32, (8, B), 1)
    sub = lax.broadcasted_iota(jnp.int32, (8, B), 0)
    n = B // 8
    rows = [a[8 * i : 8 * i + 8] for i in range(n)]
    out = []
    wide = lambda x: jnp.broadcast_to(x, (8, B))
    for q in range(n):
        k = 8 * q
        cols = [wide(rows[q][:, k + t : k + t + 1]) for t in range(8)]
        piv = [[wide(cols[j][i : i + 1, :]) if j <= i else None for j in range(8)] for i in range(8)]
        inside = (lane >= k) & (lane < k + 8)
        e = [
            jnp.where(lane == k + t, 1.0, jnp.where(inside, 0.0, wide(rows[q][t : t + 1, :])))
            for t in range(8)
        ]
        fin, s, u, ds = [None] * 8, [None] * 8, {}, []
        for t in range(0, 8, 2):
            p0, p1, p2 = piv[t][t], piv[t + 1][t], piv[t + 1][t + 1]
            rd = reciprocal(p0 * p2 - p1 * p1)
            i0, i1, i2 = p2 * rd, p1 * rd, p0 * rd
            ds.append((i0, i1, i2))
            for i in range(t + 2, 8):
                x0, x1 = piv[i][t], piv[i][t + 1]
                u[i, t] = x0 * i0 - x1 * i1
                u[i, t + 1] = x1 * i2 - x0 * i1
            for i in range(t + 2, 8):
                for j in range(t + 2, i + 1):
                    piv[i][j] = piv[i][j] - (u[i, t] * piv[j][t] + u[i, t + 1] * piv[j][t + 1])
                e[i] = e[i] - (u[i, t] * e[t] + u[i, t + 1] * e[t + 1])
            ra = lax.rsqrt(p0)
            m = p1 * ra * ra
            fin[t] = e[t] * ra
            fin[t + 1] = (e[t + 1] - m * e[t]) * lax.rsqrt(p2 - m * p1)
        if q < n - 1:
            for t in range(6, -1, -2):
                i0, i1, i2 = ds[t // 2]
                v0 = e[t] * i0 - e[t + 1] * i1
                v1 = e[t + 1] * i2 - e[t] * i1
                for i in range(7, t + 1, -1):
                    v0 = v0 - u[i, t] * s[i]
                    v1 = v1 - u[i, t + 1] * s[i]
                s[t], s[t + 1] = v0, v1
        o = fin[0]
        for t in range(1, 8):
            o = jnp.where(sub == t, fin[t], o)
        out.append(jnp.where(lane <= sub + k, o, 0.0))
        for i in range(q + 1, n):
            acc = jnp.where(inside, 0.0, rows[i])
            for t in range(8):
                acc = acc - wide(rows[i][:, k + t : k + t + 1]) * s[t]
            rows[i] = acc
    return jnp.concatenate(out, axis=0)


def factor_inverse_kernel(n, g_ref, w):
    w[...] = g_ref[...]

    def step(j, carry):
        jj = pl.multiple_of(j * B, B)
        inv = pivot_inverse(w[pl.ds(jj, B), pl.ds(jj, B)])
        w[pl.ds(jj, B), :] = jnp.dot(
            inv, w[pl.ds(jj, B), :], precision=HIGH, preferred_element_type=jnp.float32
        )
        w[pl.ds(jj, B), pl.ds(jj, B)] = inv

        def update(i, c):
            ii = pl.multiple_of(i * B, B)
            m = w[pl.ds(jj, B), pl.ds(ii, B)]
            w[pl.ds(ii, B), pl.ds(jj, B)] = jnp.zeros((B, B), jnp.float32)
            w[pl.ds(ii, B), :] = w[pl.ds(ii, B), :] - lax.dot_general(
                m,
                w[pl.ds(jj, B), :],
                (((0,), (0,)), ((), ())),
                precision=HIGH,
                preferred_element_type=jnp.float32,
            )
            return c

        lax.fori_loop(j + 1, n, update, 0)
        return carry

    lax.fori_loop(0, n, step, 0)
    for j in range(n - 1):
        w[j * B : (j + 1) * B, (j + 1) * B :] = jnp.zeros((B, (n - 1 - j) * B), jnp.float32)


def factor_inverse(gram):
    k = gram.shape[0]
    return pl.pallas_call(
        lambda *refs: factor_inverse_kernel(k // B, *refs),
        out_shape=jax.ShapeDtypeStruct((k, k), jnp.float32),
        in_specs=[pl.BlockSpec(memory_space=pltpu.VMEM)],
        out_specs=pl.BlockSpec(memory_space=pltpu.VMEM),
        compiler_params=pltpu.CompilerParams(vmem_limit_bytes=24 * 2**20),
        cost_estimate=pl.CostEstimate(flops=8 * 10**9, bytes_accessed=10**8, transcendentals=0),
    )(gram)


def dot32(a, b, dims, **kw):
    return lax.dot_general(a, b, (dims, ((), ())), preferred_element_type=jnp.float32, **kw)


def body(left_tensor, right_tensor, diag_gate, hop_gate, sketch, sector_rows, kept):
    bf16, f32 = jnp.bfloat16, jnp.float32
    left, right, diag, hop = left_tensor[0], right_tensor[0], diag_gate[0], hop_gate[0]
    rows_here, middle = left.shape
    width = sketch.shape[1]
    columns = right.shape[1]
    blk_count = lax.axis_size("blk")
    total = rows_here * blk_count
    cols_here = columns // blk_count
    groups = lax.axis_size("grp")
    me = lax.axis_index("blk")
    up = [(i, i + 1) for i in range(groups - 1)]
    down = [(i + 1, i) for i in range(groups - 1)]
    low = lambda x: lax.ppermute(x, "grp", up)
    high = lambda x: lax.ppermute(x, "grp", down)

    right_low, right_high = low(right), high(right)
    left_low, left_high = low(left), high(left)
    stack = jnp.concatenate(
        [
            right.astype(f32) * diag[None],
            right_low.astype(f32) * hop[None],
            right_high.astype(f32) * hop[None],
        ],
        axis=0,
    ).astype(bf16)
    mapped = dot32(stack, sketch, ((1,), (0,))).astype(bf16)
    mapped = lax.all_gather(mapped.reshape(3, -1, width), "blk", axis=1, tiled=True)
    wide_left = jnp.concatenate([left, left_low, left_high], axis=1)
    sketched = dot32(wide_left, mapped.reshape(-1, width), ((1,), (0,)))
    row_index = me * rows_here + jnp.arange(rows_here, dtype=jnp.int32)
    live = row_index[:, None] < sector_rows[0]
    col_live = jnp.arange(width, dtype=jnp.int32)[None, :] < kept[0]
    sketched = jnp.where(live & col_live, sketched, 0.0).astype(bf16)
    sketched_all = lax.all_gather(sketched, "blk", axis=0, tiled=True)
    gram = dot32(sketched_all, sketched_all, ((0,), (0,)))
    gram = gram + jnp.where(col_live, 0.0, 1.0) * jnp.eye(width, dtype=f32)

    left_all = lax.all_gather(left, "blk", axis=0, tiled=True)
    right_c = lax.all_to_all(right, "blk", split_axis=1, concat_axis=0, tiled=True)
    theta_c = dot32(left_all, right_c, ((1,), (0,))).astype(bf16)
    theta_low, theta_high = low(theta_c).astype(f32), high(theta_c).astype(f32)
    diag_c = lax.dynamic_slice_in_dim(diag, me * cols_here, cols_here)
    hop_c = lax.dynamic_slice_in_dim(hop, me * cols_here, cols_here)
    mixed_c = diag_c[None] * theta_c.astype(f32) + hop_c[None] * (theta_low + theta_high)
    all_live = jnp.arange(total, dtype=jnp.int32)[:, None] < sector_rows[0]
    mixed_c = jnp.where(all_live, mixed_c, 0.0).astype(bf16)
    projected = dot32(mixed_c, sketched_all, ((0,), (0,)))

    inverse = factor_inverse(gram)
    scale = math.sqrt(total)
    left_out = dot32(sketched.astype(f32), inverse, ((1,), (1,)), precision=HIGH) * scale
    right_out = dot32(projected, inverse, ((1,), (1,)), precision=HIGH) / scale
    return (left_out[None], right_out[:, None, :])


def solution(mesh):
    in_specs = (
        P("grp", "blk", None),
        P("grp", "blk", None),
        P("grp", None),
        P("grp", None),
        P(),
        P("grp"),
        P("grp"),
    )
    out_specs = (P("grp", "blk", None), P("blk", "grp", None))
    return jax.shard_map(body, mesh=mesh, in_specs=in_specs, out_specs=out_specs, check_vma=False)
```

time: 572 us -> 253 us (0.44)
  other arithmetic: 214 us -> 1.87 us
  waiting for transfers between devices: 243 us -> 145 us
  local copies, waits for them, and re-layouts: 51.9 us -> 3.56 us
  Pallas kernels: 0 us -> 39.7 us
  starting transfers between devices: 3.22 us -> 18.9 us
  matrix products: 34.4 us -> 26.8 us
    another operation x26 -> x2, other arithmetic: 206 us -> 1.84 us  [the longest x22 143 us: body(): factor = jnp.linalg.cholesky(gram_mat)]
    psum x1 -> x0, waiting for transfers between devices: 103 us -> none  [body(): gram_mat = lax.psum(gram_local, 'blk')]
    unnamed x4 -> x3, waiting for transfers between devices: 77.5 us -> 0.73 us
    all_gather x1 -> x3, waiting for transfers between devices: 58.6 us -> 130 us  [the longest x1 49.1 us: body(): sketched_all = lax.all_gather(sketched, 'blk', axis=0, tiled=True)]
    pallas_call x0 -> x1, Pallas kernels: none -> 39.7 us  [factor_inverse(): pl.pallas_call(lambda *refs: factor_inverse_kernel(k // B, *refs), out_sh...]
    another operation x51 -> x0, local copies, waits for them, and re-layouts: 37.4 us -> none
    another operation x21 -> x0, matrix products: 24.3 us -> none  [the longest x10 16.2 us: body(): factor = jnp.linalg.cholesky(gram_mat)]
    dot_general x4 -> x7, matrix products: 10.1 us -> 26.8 us  [dot32(): lax.dot_general(a, b, (dims, ((), ())), preferred_element_type=jnp.float3...]
  transfers between devices with their start and end apart: 5 -> 10, of which waited for: 4 -> 6; matrix products, arithmetic and copies ran while one was open for 0% -> 8% of each run, Pallas kernels for 0% -> 16%
where the time goes in v1:
time: 253 us; the launch traced here: 251 us
  waiting for transfers between devices  145 us (57%)
  Pallas kernels  39.7 us (16%)
  matrix products  26.8 us (11%)
  starting transfers between devices  18.9 us (7%)
  between operations  15.3 us (6%)
  local copies, waits for them, and re-layouts  3.56 us (1%)
    all_gather x1, waiting for transfers between devices, body(): sketched_all = lax.all_gather(sketched, 'blk', axis=0, tiled=True)  49.1 us
    all_gather x1, waiting for transfers between devices, body(): lax.all_gather(mapped.reshape(3, -1, width), 'blk', axis=1, tiled=True)  44.6 us
    pallas_call x1, Pallas kernels, factor_inverse(): pl.pallas_call(lambda *refs: factor_inverse_kernel(k // B, *refs), out_sh...  39.7 us
    all_gather x1, waiting for transfers between devices, body(): left_all = lax.all_gather(left, 'blk', axis=0, tiled=True)  35.9 us
    dot_general x7, matrix products, dot32(): lax.dot_general(a, b, (dims, ((), ())), preferred_element_type=jnp.float3...  26.8 us
    all_to_all x1, waiting for transfers between devices, body(): lax.all_to_all(right, 'blk', split_axis=1, concat_axis=0, tiled=True)  10.6 us
    ppermute x3, starting transfers between devices, body(): low = lambda x: lax.ppermute(x, 'grp', up)  10.1 us
  transfers between devices with their start and end apart: 10, of which 6 were waited for; matrix products, arithmetic and copies ran while one was open for 8% of the time, Pallas kernels for 16%

profile of v1, /device:TPU:0, one launch (start us, length us, event | category | flops | bytes accessed | tf_op | source)
XLA Modules:
  0.0 251.3 jit_solution(17454392525511280886)
XLA Ops:
  7.2 0.0 all-gather.5.cloned.1.call-start
  7.2 1.3 collective-permute-start.2
  8.5 1.3 collective-permute-start.3
  9.8 1.0 multiply_convert_fusion.2
  10.9 0.0 collective-permute-done.2
  10.9 3.6 %collective-permute-done.3 = bf16[48,3072]{1,0:T(8,128)(2,1)S(1)} collective-permute-done((bf16[48,3072]{1,0:T(8,128)(2,1)}, bf16[48,3072]{1,0:T(8,128)(2,1)S(1)}, u32[]{:S(2)}, u32[]{:S(2)}) %collective-permute-start.3) | collective-permute-done | bytes 294944 | tf_op jit(solution)/shard_map/ppermute | solution.py:136
  14.4 0.8 multiply_convert_fusion.1
  15.3 0.0 copy-start.2
  15.3 3.9 %convolution_convert_fusion = bf16[144,768]{1,0:T(8,128)(2,1)} fusion(bf16[3072,768]{1,0:T(8,128)(2,1)} %param.11, bf16[48,3072]{1,0:T(8,128)(2,1)S(1)} %get-tuple-element.7, bf16[48,3072]{1,0:T(8,128)(2,1)S(1)} %get-tuple-element.6, bf16[48,3072]{1,0:T(8,128)(2,1)S(1)} %multiply_convert_fusion.2), kind=kOutput, calls=%fused_computation.12 | convolution fusion | flops 682242048 | bytes 5824512 | tf_op jit(solution)/shard_map/dot_general | solution.py:119
  19.2 0.0 all-gather.5.cloned.1.call-update
  19.2 0.0 all-gather.9.cloned.1.call-start
  19.3 0.7 all-gather.9.cloned.1.call-update
  20.0 0.0 all-gather.7.cloned.1.call-start
  20.0 0.0 copy-done.2
  20.0 7.0 %collective-permute-start = (bf16[192,768]{1,0:T(8,128)(2,1)S(1)}, bf16[192,768]{1,0:T(8,128)(2,1)S(1)}, u32[]{:S(2)}, u32[]{:S(2)}) collective-permute-start(bf16[192,768]{1,0:T(8,128)(2,1)S(1)} %bitcast.40), channel_id=1, source_target_pairs={{0,16},{16,32},{32,48},{48,64},{64,80},{80,96},{96,112},{1,17},{17... | collective-permute-start | bytes 884744 | tf_op jit(solution)/shard_map/ppermute | solution.py:135
  27.0 1.3 collective-permute-start.1
  29.7 0.0 collective-permute-done
  29.7 0.8 collective-permute-done.1
  30.5 44.6 %all-gather.5.cloned.1.call-done = bf16[3,768,768]{2,1,0:T(8,128)(2,1)} async-done(((bf16[3,48,768]{2,1,0:T(8,128)(2,1)}), bf16[3,768,768]{2,1,0:T(8,128)(2,1)}) %all-gather.5.cloned.1.call-update) | async-done | bytes 3538960 | tf_op jit(solution)/shard_map/all_gather | solution.py:149
  75.1 0.0 copy-start.1
  75.1 3.6 %fusion.7 = bf16[192,768]{1,0:T(8,128)(2,1)} fusion(bf16[2304,768]{1,0:T(8,128)(2,1)} %bitcast.50, bf16[192,768]{1,0:T(8,128)(2,1)S(1)} %collective-permute-done.1, bf16[192,768]{1,0:T(8,128)(2,1)S(1)} %collective-permute-done, bf16[192,768]{1,0:T(8,128)(2,1)S(1)} %bitcast.42, pred[768]{0:T(1024)(128)(4,1)S(1)} %iota_compare_fusion.2, ...), kind=kOutput, calls=%fused_computation.11 | convolution fusion | flops 682573824 | bytes 4719552 | tf_op jit(solution)/shard_map/dot_general | solution.py:119
  78.7 0.0 all-gather.7.cloned.1.call-update
  78.8 0.0 copy-done.1
  78.8 0.5 all_to_all.14
  79.2 0.9 copy.10
  80.1 4.6 %all-to-all-start = ((bf16[48,16,192]{2,0,1:T(8,128)(2,1)}), bf16[48,16,192]{2,0,1:T(8,128)(2,1)S(1)}, u32[]{:S(2)}, u32[]{:S(2)}) async-start(bf16[48,16,192]{2,0,1:T(8,128)(2,1)} %copy.10), calls=%async_computation | async-start | bytes 786432 | tf_op jit(solution)/shard_map/all_to_all | solution.py:161
  84.7 0.8 constant_dynamic-slice_fusion
  85.5 10.6 %all-to-all-done = bf16[48,16,192]{2,0,1:T(8,128)(2,1)S(1)} async-done(((bf16[48,16,192]{2,0,1:T(8,128)(2,1)}), bf16[48,16,192]{2,0,1:T(8,128)(2,1)S(1)}, u32[]{:S(2)}, u32[]{:S(2)}) %all-to-all-start) | async-done | bytes 294944 | tf_op jit(solution)/shard_map/all_to_all | solution.py:161
  96.1 35.9 %all-gather.9.cloned.1.call-done = bf16[1,3072,768]{2,1,0:T(8,128)(2,1)} async-done(((bf16[1,192,768]{2,1,0:T(8,128)(2,1)}), bf16[1,3072,768]{2,1,0:T(8,128)(2,1)}) %all-gather.9.cloned.1.call-update) | async-done | bytes 4718608 | tf_op jit(solution)/shard_map/all_gather | solution.py:160
  132.0 4.0 %fusion.2 = bf16[3072,192]{0,1:T(8,128)(2,1)S(1)} fusion(bf16[768,192]{1,0:T(8,128)(2,1)S(1)} %bitcast.37, bf16[1,3072,768]{2,1,0:T(8,128)(2,1)} %all-gather.9.cloned.1.call-done), kind=kOutput, calls=%fused_computation.2 | convolution fusion | flops 906559488 | bytes 6193152 | tf_op jit(solution)/shard_map/dot_general | solution.py:119
  136.0 1.8 collective-permute-start.4
  137.8 1.5 collective-permute-start.5
  139.3 49.1 %all-gather.7.cloned.1.call-done = bf16[3072,768]{1,0:T(8,128)(2,1)} async-done(((bf16[192,768]{1,0:T(8,128)(2,1)}), bf16[3072,768]{1,0:T(8,128)(2,1)}) %all-gather.7.cloned.1.call-update) | async-done | bytes 4718608 | tf_op jit(solution)/shard_map/all_gather | solution.py:156
  188.4 0.0 slice-start
  188.4 7.8 %select_add_fusion.refs_0_ = f32[768,768]{1,0:T(8,128)S(1)} fusion(bf16[3072,768]{1,0:T(8,128)(2,1)} %all-gather.7.cloned.1.call-done, f32[768]{0:T(1024)S(1)} %broadcast_select_fusion), kind=kOutput, calls=%fused_computation.4 | convolution fusion | flops 3625648128 | bytes 7080960 | tf_op jit(solution)/shard_map/dot_general | solution.py:119
  196.2 0.0 copy-start
  196.2 0.0 slice-start.1
  196.2 39.7 %shard_map.86 = f32[768,768]{1,0:T(8,128)S(1)} custom-call(f32[768,768]{1,0:T(8,128)S(1)} %select_add_fusion.refs_0_), custom_call_target="tpu_custom_call" | custom-call | flops 8000000000 | bytes 100000000 | tf_op jit(solution)/shard_map/pallas_call | solution.py:108
  235.9 0.0 copy-done
  235.9 2.3 fusion.6
  238.2 0.0 collective-permute-done.4
  238.2 0.0 collective-permute-done.5
  238.2 0.0 slice-done
  238.2 0.0 slice-done.1
  238.2 2.7 %fusion.8 = f32[192,768]{1,0:T(8,128)S(1)} fusion(bf16[3072,768]{1,0:T(8,128)(2,1)S(1)} %bitcast.49, bf16[3072,192]{0,1:T(8,128)(2,1)} %collective-permute-done.5, bf16[3072,192]{0,1:T(8,128)(2,1)S(1)} %collective-permute-done.4, bf16[3072,192]{0,1:T(8,128)(2,1)S(1)} %fusion.2, f32[192]{0:T(256)S(1)} %bitcast.46, f32[192]{0:T(256)S(1)} %bitcast.47, ...), kind=kOutput, calls=%fused_computation.13 | convolution fusion | flops 911278080 | bytes 8851968 | tf_op jit(solution)/shard_map/dot_general | solution.py:119
  240.9 2.5 fusion.5
  243.4 1.4 copy.11
  (5 shorter events, 0.0 us)
Async XLA Ops:
  7.2 68.0 %all-gather.5.cloned.1.call-start = ((), (), s32[]{:S(2)}) async-start(), calls=%async_computation.1 | async-start | bytes 3760128 | tf_op jit(solution)/shard_map/all_gather | solution.py:149
  7.2 3.7 %collective-permute-start.2 = (bf16[48,3072]{1,0:T(8,128)(2,1)}, bf16[48,3072]{1,0:T(8,128)(2,1)S(1)}, u32[]{:S(2)}, u32[]{:S(2)}) collective-permute-start(bf16[48,3072]{1,0:T(8,128)(2,1)} %bitcast.38), channel_id=1, source_target_pairs={{0,16},{16,32},{32,48},{48,64},{64,80},{80,96},{96,112},{1,17},{17... | collective-permute-start | bytes 884744 | tf_op jit(solution)/shard_map/ppermute | solution.py:135
  8.5 5.9 %collective-permute-start.3 = (bf16[48,3072]{1,0:T(8,128)(2,1)}, bf16[48,3072]{1,0:T(8,128)(2,1)S(1)}, u32[]{:S(2)}, u32[]{:S(2)}) collective-permute-start(bf16[48,3072]{1,0:T(8,128)(2,1)} %bitcast.39), channel_id=1, source_target_pairs={{16,0},{32,16},{48,32},{64,48},{80,64},{96,80},{112,96},{17,1},{33... | collective-permute-start | bytes 884744 | tf_op jit(solution)/shard_map/ppermute | solution.py:136
  15.3 4.8 %copy-start.2 = (bf16[1,192,768]{2,1,0:T(8,128)(2,1)S(1)}, bf16[1,192,768]{2,1,0:T(8,128)(2,1)}, u32[]{:S(2)}) copy-start(bf16[1,192,768]{2,1,0:T(8,128)(2,1)} %param.7) | copy-start | bytes 884740
  19.2 112.8 %all-gather.9.cloned.1.call-start = ((), (), s32[]{:S(2)}) async-start(), calls=%async_computation.3 | async-start | bytes 5013504 | tf_op jit(solution)/shard_map/all_gather | solution.py:160
  20.0 168.4 %all-gather.7.cloned.1.call-start = ((), (), s32[]{:S(2)}) async-start(), calls=%async_computation.2 | async-start | bytes 5013504 | tf_op jit(solution)/shard_map/all_gather | solution.py:156
  20.0 9.6 %collective-permute-start = (bf16[192,768]{1,0:T(8,128)(2,1)S(1)}, bf16[192,768]{1,0:T(8,128)(2,1)S(1)}, u32[]{:S(2)}, u32[]{:S(2)}) collective-permute-start(bf16[192,768]{1,0:T(8,128)(2,1)S(1)} %bitcast.40), channel_id=1, source_target_pairs={{0,16},{16,32},{32,48},{48,64},{64,80},{80,96},{96,112},{1,17},{17... | collective-permute-start | bytes 884744 | tf_op jit(solution)/shard_map/ppermute | solution.py:135
  27.0 3.5 %collective-permute-start.1 = (bf16[192,768]{1,0:T(8,128)(2,1)S(1)}, bf16[192,768]{1,0:T(8,128)(2,1)S(1)}, u32[]{:S(2)}, u32[]{:S(2)}) collective-permute-start(bf16[192,768]{1,0:T(8,128)(2,1)S(1)} %bitcast.41), channel_id=1, source_target_pairs={{16,0},{32,16},{48,32},{64,48},{80,64},{96,80},{112,96},{17,1},{33... | collective-permute-start | bytes 884744 | tf_op jit(solution)/shard_map/ppermute | solution.py:136
  75.1 3.6 %copy-start.1 = (bf16[1,48,3072]{2,1,0:T(8,128)(2,1)S(1)}, bf16[1,48,3072]{2,1,0:T(8,128)(2,1)}, u32[]{:S(2)}) copy-start(bf16[1,48,3072]{2,1,0:T(8,128)(2,1)} %param.8) | copy-start | bytes 884740
  80.1 16.0 %all-to-all-start = ((bf16[48,16,192]{2,0,1:T(8,128)(2,1)}), bf16[48,16,192]{2,0,1:T(8,128)(2,1)S(1)}, u32[]{:S(2)}, u32[]{:S(2)}) async-start(bf16[48,16,192]{2,0,1:T(8,128)(2,1)} %copy.10), calls=%async_computation | async-start | bytes 786432 | tf_op jit(solution)/shard_map/all_to_all | solution.py:161
  136.0 102.2 %collective-permute-start.4 = (bf16[3072,192]{0,1:T(8,128)(2,1)S(1)}, bf16[3072,192]{0,1:T(8,128)(2,1)S(1)}, u32[]{:S(2)}, u32[]{:S(2)}) collective-permute-start(bf16[3072,192]{0,1:T(8,128)(2,1)S(1)} %fusion.2), channel_id=1, source_target_pairs={{0,16},{16,32},{32,48},{48,64},{64,80},{80,96},{96,112},{1,17},{17... | collective-permute-start | bytes 3538952 | tf_op jit(solution)/shard_map/ppermute | solution.py:135
  137.8 100.4 %collective-permute-start.5 = (bf16[3072,192]{0,1:T(8,128)(2,1)S(1)}, bf16[3072,192]{0,1:T(8,128)(2,1)}, u32[]{:S(2)}, u32[]{:S(2)}) collective-permute-start(bf16[3072,192]{0,1:T(8,128)(2,1)S(1)} %fusion.2), channel_id=1, source_target_pairs={{16,0},{32,16},{48,32},{64,48},{80,64},{96,80},{112,96},{17,1},{33... | collective-permute-start | bytes 3538952 | tf_op jit(solution)/shard_map/ppermute | solution.py:136
  188.4 49.8 %slice-start = ((s8[4718592]{0:T(1024)(128)(4,1)}), s8[4194304]{0:T(1024)(128)(4,1)S(1)}, s32[]{:S(2)}) async-start(s8[4718592]{0:T(1024)(128)(4,1)} %bitcast.48), calls=%async_computation.4 | async-start | bytes 8388608
  196.2 39.7 %copy-start = (bf16[192,768]{1,0:T(8,128)(2,1)S(1)}, bf16[192,768]{1,0:T(8,128)(2,1)}, u32[]{:S(2)}) copy-start(bf16[192,768]{1,0:T(8,128)(2,1)} %fusion.7) | copy-start | bytes 884740
  196.2 42.0 %slice-start.1 = ((s8[4718592]{0:T(1024)(128)(4,1)}), s8[524288]{0:T(1024)(128)(4,1)S(1)}, s32[]{:S(2)}) async-start(s8[4718592]{0:T(1024)(128)(4,1)} %bitcast.48), calls=%async_computation.5 | async-start | bytes 1048576
Sparse Core Ops, SparseCore 0:
  19.3 55.7 all-gather.4
  77.3 54.6 all-gather.8
  134.7 53.5 all-gather.6

commit v2 on v1

--- a/solution.py
+++ b/solution.py
@@ -71,8 +71,26 @@
     return jnp.concatenate(out, axis=0)
 
 
-def factor_inverse_kernel(n, g_ref, w):
-    w[...] = g_ref[...]
+def factor_inverse_kernel(n, s_ref, dead_ref, w):
+    eye = lax.broadcasted_iota(jnp.int32, (B, B), 0) == lax.broadcasted_iota(jnp.int32, (B, B), 1)
+    for j in range(n):
+        if j:
+            w[j * B : (j + 1) * B, : j * B] = jnp.zeros((B, j * B), jnp.float32)
+        block = s_ref[:, j * B : (j + 1) * B]
+
+        def gram(i, c, block=block):
+            ii = pl.multiple_of(i * B, B)
+            w[pl.ds(j * B, B), pl.ds(ii, B)] = lax.dot_general(
+                block,
+                s_ref[:, pl.ds(ii, B)],
+                (((0,), (0,)), ((), ())),
+                preferred_element_type=jnp.float32,
+            )
+            return c
+
+        lax.fori_loop(j, n, gram, 0)
+        here = slice(j * B, (j + 1) * B)
+        w[here, here] = w[here, here] + jnp.where(eye, dead_ref[:, here], 0.0)
 
     def step(j, carry):
         jj = pl.multiple_of(j * B, B)
@@ -103,20 +121,271 @@
         w[j * B : (j + 1) * B, (j + 1) * B :] = jnp.zeros((B, (n - 1 - j) * B), jnp.float32)
 
 
-def factor_inverse(gram):
-    k = gram.shape[0]
+def factor_inverse(sketched, dead):
+    k = sketched.shape[1]
     return pl.pallas_call(
         lambda *refs: factor_inverse_kernel(k // B, *refs),
         out_shape=jax.ShapeDtypeStruct((k, k), jnp.float32),
-        in_specs=[pl.BlockSpec(memory_space=pltpu.VMEM)],
+        in_specs=[pl.BlockSpec(memory_space=pltpu.VMEM)] * 2,
         out_specs=pl.BlockSpec(memory_space=pltpu.VMEM),
-        compiler_params=pltpu.CompilerParams(vmem_limit_bytes=24 * 2**20),
-        cost_estimate=pl.CostEstimate(flops=8 * 10**9, bytes_accessed=10**8, transcendentals=0),
-    )(gram)
+        compiler_params=pltpu.CompilerParams(vmem_limit_bytes=32 * 2**20),
+        cost_estimate=pl.CostEstimate(
+            flops=20 * 10**9, bytes_accessed=10**8, transcendentals=0
+        ),
+    )(sketched, dead)
 
 
 def dot32(a, b, dims, **kw):
     return lax.dot_general(a, b, (dims, ((), ())), preferred_element_type=jnp.float32, **kw)
+
+
+SIDE = 4
+SK_PARTS = 2
+
+
+def gather_kernel(
+    right, left, gates, sketch_hbm, rowm, colm, pieces,
+    sk_out, pieces_out,
+    sketch, mapped, right_n, left_n, total,
+    load_sem, x_send, x_recv, m_send, m_recv, s_send, s_recv, a_send, a_recv, n_send, n_recv,
+):
+    bf16, f32 = jnp.bfloat16, jnp.float32
+    g = lax.axis_index("grp")
+    me = lax.axis_index("blk")
+    groups = lax.axis_size("grp")
+    blks = SIDE * SIDE
+    cx, cy = me // SIDE, me % SIDE
+    depth = right.shape[0]
+    rows, width = sk_out.shape[1], sk_out.shape[2]
+    half_w = width // 2
+
+    load = pltpu.make_async_copy(sketch_hbm, sketch, load_sem)
+    load.start()
+    keep = pltpu.make_async_copy(pieces.at[me], pieces_out.at[0, me], a_recv.at[me])
+    keep.start()
+
+    barrier = pltpu.get_barrier_semaphore()
+    peers = [{"blk": lax.rem(me + i, blks)} for i in range(1, blks)]
+    up = {"grp": lax.rem(g + 1, groups)}
+    down = {"grp": lax.rem(g + groups - 1, groups)}
+    for peer in peers + [up, down]:
+        pl.semaphore_signal(barrier, inc=1, device_id=peer, device_id_type=pl.DeviceIdType.MESH)
+    pl.semaphore_wait(barrier, len(peers) + 2)
+
+    def remote(src, dst, send, recv, to):
+        return pltpu.make_async_remote_copy(
+            src_ref=src, dst_ref=dst, send_sem=send, recv_sem=recv,
+            device_id=to, device_id_type=pl.DeviceIdType.MESH,
+        )
+
+    started = []
+
+    def go(copy):
+        copy.start()
+        started.append(copy)
+
+    for slot, to in ((0, up), (1, down)):
+        go(remote(right, right_n.at[slot], x_send.at[slot], x_recv.at[slot], to))
+    for slot, to in ((0, up), (1, down)):
+        go(remote(left, left_n.at[slot], x_send.at[2 + slot], x_recv.at[2 + slot], to))
+    for i in range(1, blks):
+        to = lax.rem(me + i, blks)
+        go(remote(pieces.at[to], pieces_out.at[0, me], a_send.at[i], a_recv.at[me], {"blk": to}))
+
+    def ring(view, send, recv):
+        count = [0]
+
+        def coords(half):
+            return (cx, cy) if half == 0 else (cy, cx)
+
+        def index(half, a, b):
+            return a * SIDE + b if half == 0 else b * SIDE + a
+
+        def owner(half, r1, r2):
+            c1, c2 = coords(half)
+            return index(half, lax.rem(c1 + r1, SIDE), lax.rem(c2 + r2, SIDE))
+
+        def ship(half, block, axis, step):
+            to = owner(half, step, 0) if axis == 0 else owner(half, 0, step)
+            ref = view(block, half)
+            go(remote(ref, ref, send.at[count[0]], recv.at[half, block], {"blk": to}))
+            count[0] += 1
+
+        def take(half, r1, r2):
+            block = owner(half, r1, r2)
+            ref = view(block, half)
+            remote(ref, ref, send.at[0], recv.at[half, block], up).wait_recv()
+            return block
+
+        plus = (0, 3)
+
+        def relay(half, r1):
+            low = take(half, r1, 3)
+            if r1 in plus:
+                ship(half, low, 1, 1)
+            high = take(half, r1, 1)
+            if r1 not in plus:
+                ship(half, high, 1, 3)
+
+        def spread(half, block):
+            ship(half, block, 1, 1)
+            ship(half, block, 1, 3)
+
+        def first():
+            for half in range(2):
+                ship(half, me, 0, 1)
+                ship(half, me, 0, 3)
+            for half in range(2):
+                spread(half, me)
+
+        def second():
+            for half in range(2):
+                b = take(half, 3, 0)
+                if half == 0:
+                    ship(half, b, 0, 1)
+                spread(half, b)
+                b = take(half, 1, 0)
+                if half == 1:
+                    ship(half, b, 0, 3)
+                spread(half, b)
+            for half in range(2):
+                relay(half, 0)
+
+        def third():
+            for half in range(2):
+                spread(half, take(half, 2, 0))
+            for half in range(2):
+                relay(half, 3)
+                relay(half, 1)
+
+        def fourth():
+            for half in range(2):
+                relay(half, 2)
+
+        def last():
+            for half in range(2):
+                for r1 in (0, 3, 1, 2):
+                    take(half, r1, 2)
+
+        return first, second, third, fourth, last
+
+    def tiles(n, f):
+        lax.fori_loop(0, n, lambda i, c: (f(i), c)[1], 0)
+
+    maps = []
+    for part in range(3):
+        view = lambda o, half, part=part: mapped.at[part, o, :, pl.ds(half * half_w, half_w)]
+        maps.append(ring(view, m_send.at[part], m_recv.at[part]))
+
+    def x_wait(ref, k):
+        remote(ref, ref, x_send.at[k], x_recv.at[k], up).wait_recv()
+
+    for part in range(3):
+        if part == 0:
+            load.wait()
+            block = right[...]
+        else:
+            x_wait(right_n.at[part - 1], part - 1)
+            block = right_n[part - 1]
+        scaled = (block.astype(f32) * gates[pl.ds(part, 1), :]).astype(bf16)
+
+        def tile(i, scaled=scaled, part=part):
+            at = pl.ds(pl.multiple_of(i * 256, 256), 256)
+            mapped[part, me, :, at] = jnp.dot(
+                scaled, sketch[:, at], preferred_element_type=f32
+            ).astype(bf16)
+
+        tiles(width // 256, tile)
+        maps[part][0]()
+    for stage in range(1, 4):
+        for part in range(3):
+            maps[part][stage]()
+    for part in range(3):
+        if part == 0:
+            block = left[...]
+        else:
+            x_wait(left_n.at[part - 1], part + 1)
+            block = left_n[part - 1]
+        maps[part][4]()
+
+        def tile(i, block=block, part=part):
+            at = pl.ds(pl.multiple_of(i * 256, 256), 256)
+            add = jnp.dot(
+                block, mapped[part, :, :, at].reshape(blks * depth, 256), preferred_element_type=f32
+            )
+            if part == 0:
+                total[:, at] = add
+            elif part == 1:
+                total[:, at] = total[:, at] + add
+            else:
+                sk_out[me, :, at] = ((total[:, at] + add) * rowm[...] * colm[:, at]).astype(bf16)
+
+        tiles(width // 256, tile)
+
+    rings = []
+    part_rows = rows // SK_PARTS
+    for part in range(SK_PARTS):
+        view = lambda o, half, part=part: sk_out.at[
+            o, pl.ds(part * part_rows, part_rows), pl.ds(half * half_w, half_w)
+        ]
+        rings.append(ring(view, s_send.at[part], s_recv.at[part]))
+    for r in rings:
+        r[0]()
+    keep.wait()
+    for i in range(1, blks):
+        o = lax.rem(me + i, blks)
+        ref = pieces_out.at[0, o]
+        remote(ref, ref, a_send.at[i], a_recv.at[o], up).wait_recv()
+    for slot, to in ((0, up), (1, down)):
+        go(remote(pieces_out.at[0], pieces_out.at[1 + slot], n_send.at[slot], n_recv.at[slot], to))
+    for stage in range(1, 5):
+        for r in rings:
+            r[stage]()
+    for slot in range(2):
+        ref = pieces_out.at[1 + slot]
+        remote(ref, ref, n_send.at[slot], n_recv.at[slot], up).wait_recv()
+    for copy in started:
+        copy.wait_send()
+
+
+def gather_sketched(right, left, gates, sketch, rowm, colm, pieces):
+    bf16, f32 = jnp.bfloat16, jnp.float32
+    rows, middle = left.shape
+    depth, columns = right.shape
+    width = sketch.shape[1]
+    blks = SIDE * SIDE
+    vmem = pl.BlockSpec(memory_space=pltpu.VMEM)
+    dma = pltpu.SemaphoreType.DMA
+    return pl.pallas_call(
+        gather_kernel,
+        out_shape=(
+            jax.ShapeDtypeStruct((blks, rows, width), bf16),
+            jax.ShapeDtypeStruct((3,) + pieces.shape, bf16),
+        ),
+        in_specs=[vmem, vmem, vmem, pl.BlockSpec(memory_space=pl.ANY), vmem, vmem, vmem],
+        out_specs=(vmem, vmem),
+        scratch_shapes=[
+            pltpu.VMEM((columns, width), bf16),
+            pltpu.VMEM((3, blks, depth, width), bf16),
+            pltpu.VMEM((2, depth, columns), bf16),
+            pltpu.VMEM((2, rows, middle), bf16),
+            pltpu.VMEM((rows, width), f32),
+            dma(()),
+            dma((4,)),
+            dma((4,)),
+            dma((3, 30)),
+            dma((3, 2, blks)),
+            dma((SK_PARTS, 30)),
+            dma((SK_PARTS, 2, blks)),
+            dma((blks,)),
+            dma((blks,)),
+            dma((2,)),
+            dma((2,)),
+        ],
+        compiler_params=pltpu.CompilerParams(
+            collective_id=0, has_side_effects=True, vmem_limit_bytes=48 * 2**20
+        ),
+    )(right, left, gates, sketch, rowm, colm, pieces)
 
 
 def body(left_tensor, right_tensor, diag_gate, hop_gate, sketch, sector_rows, kept):
@@ -124,52 +393,37 @@
     left, right, diag, hop = left_tensor[0], right_tensor[0], diag_gate[0], hop_gate[0]
     rows_here, middle = left.shape
     width = sketch.shape[1]
-    columns = right.shape[1]
-    blk_count = lax.axis_size("blk")
-    total = rows_here * blk_count
-    cols_here = columns // blk_count
-    groups = lax.axis_size("grp")
-    me = lax.axis_index("blk")
-    up = [(i, i + 1) for i in range(groups - 1)]
-    down = [(i + 1, i) for i in range(groups - 1)]
-    low = lambda x: lax.ppermute(x, "grp", up)
-    high = lambda x: lax.ppermute(x, "grp", down)
-
-    right_low, right_high = low(right), high(right)
-    left_low, left_high = low(left), high(left)
-    stack = jnp.concatenate(
+    depth, columns = right.shape
+    blks = lax.axis_size("blk")
+    total = rows_here * blks
+    cols_here = columns // blks
+    g, me = lax.axis_index("grp"), lax.axis_index("blk")
+    hop_low = jnp.where(g > 0, hop, 0.0)
+    hop_high = jnp.where(g < lax.axis_size("grp") - 1, hop, 0.0)
+    gates = jnp.stack([diag, hop_low, hop_high])
+    row_index = me * rows_here + jnp.arange(rows_here, dtype=jnp.int32)
+    rowm = (row_index[:, None] < sector_rows[0]).astype(f32)
+    colm = (jnp.arange(width, dtype=jnp.int32)[None, :] < kept[0]).astype(f32)
+    pieces = jnp.concatenate(
         [
-            right.astype(f32) * diag[None],
-            right_low.astype(f32) * hop[None],
-            right_high.astype(f32) * hop[None],
+            right.reshape(depth, blks, cols_here).transpose(1, 0, 2),
+            left.T.reshape(blks, depth, rows_here),
         ],
-        axis=0,
-    ).astype(bf16)
-    mapped = dot32(stack, sketch, ((1,), (0,))).astype(bf16)
-    mapped = lax.all_gather(mapped.reshape(3, -1, width), "blk", axis=1, tiled=True)
-    wide_left = jnp.concatenate([left, left_low, left_high], axis=1)
-    sketched = dot32(wide_left, mapped.reshape(-1, width), ((1,), (0,)))
-    row_index = me * rows_here + jnp.arange(rows_here, dtype=jnp.int32)
-    live = row_index[:, None] < sector_rows[0]
-    col_live = jnp.arange(width, dtype=jnp.int32)[None, :] < kept[0]
-    sketched = jnp.where(live & col_live, sketched, 0.0).astype(bf16)
-    sketched_all = lax.all_gather(sketched, "blk", axis=0, tiled=True)
-    gram = dot32(sketched_all, sketched_all, ((0,), (0,)))
-    gram = gram + jnp.where(col_live, 0.0, 1.0) * jnp.eye(width, dtype=f32)
-
-    left_all = lax.all_gather(left, "blk", axis=0, tiled=True)
-    right_c = lax.all_to_all(right, "blk", split_axis=1, concat_axis=0, tiled=True)
-    theta_c = dot32(left_all, right_c, ((1,), (0,))).astype(bf16)
-    theta_low, theta_high = low(theta_c).astype(f32), high(theta_c).astype(f32)
-    diag_c = lax.dynamic_slice_in_dim(diag, me * cols_here, cols_here)
-    hop_c = lax.dynamic_slice_in_dim(hop, me * cols_here, cols_here)
-    mixed_c = diag_c[None] * theta_c.astype(f32) + hop_c[None] * (theta_low + theta_high)
-    all_live = jnp.arange(total, dtype=jnp.int32)[:, None] < sector_rows[0]
-    mixed_c = jnp.where(all_live, mixed_c, 0.0).astype(bf16)
-    projected = dot32(mixed_c, sketched_all, ((0,), (0,)))
-
-    inverse = factor_inverse(gram)
+        axis=1,
+    )
+    sk, got = gather_sketched(right, left, gates, sketch, rowm, colm, pieces)
+    sketched_all = sk.reshape(total, width)
+    left_c = got[:, :, depth:, :].transpose(0, 2, 1, 3).reshape(3 * depth, total)
+    joint = dot32(left_c, sketched_all, ((1,), (0,))).astype(bf16)
+    joint = lax.all_gather(joint.reshape(3, depth, width), "blk", axis=1, tiled=True)
+    inverse = factor_inverse(sketched_all, 1.0 - colm)
+
+    gates_c = lax.dynamic_slice_in_dim(gates, me * cols_here, cols_here, axis=1)
+    right_c = got[:, :, :depth, :].reshape(3, middle, cols_here)
+    right_c = (right_c.astype(f32) * gates_c[:, None, :]).astype(bf16)
+    projected = dot32(right_c.reshape(3 * middle, cols_here), joint.reshape(3 * middle, width), ((0,), (0,)))
     scale = math.sqrt(total)
+    sketched = lax.dynamic_index_in_dim(sk, me, 0, keepdims=False)
     left_out = dot32(sketched.astype(f32), inverse, ((1,), (1,)), precision=HIGH) * scale
     right_out = dot32(projected, inverse, ((1,), (1,)), precision=HIGH) / scale
     return (left_out[None], right_out[:, None, :])

time: 253 us -> 162 us (0.64)
  waiting for transfers between devices: 145 us -> 0.02 us
  Pallas kernels: 39.7 us -> 120 us
  starting transfers between devices: 18.9 us -> 0.04 us
  matrix products: 26.8 us -> 12.1 us
  local copies, waits for them, and re-layouts: 3.56 us -> 11.4 us
    all_gather x3 -> x1, waiting for transfers between devices: 130 us -> 0.01 us  [body(): lax.all_gather(joint.reshape(3, depth, width), 'blk', axis=1, tiled=True)]
    pallas_call x0 -> x1, Pallas kernels: none -> 71.4 us  [gather_sketched(): pl.pallas_call(gather_kernel, out_shape=(jax.ShapeDtypeStruct((blks, rows...]
    dot_general x7 -> x4, matrix products: 26.8 us -> 12.1 us  [dot32(): lax.dot_general(a, b, (dims, ((), ())), preferred_element_type=jnp.float3...]
    ppermute x6 -> x0, starting transfers between devices: 14.2 us -> none  [the longest x3 10.1 us: body(): low = lambda x: lax.ppermute(x, 'grp', up)]
    all_to_all x1 -> x0, waiting for transfers between devices: 10.6 us -> none  [body(): lax.all_to_all(right, 'blk', split_axis=1, concat_axis=0, tiled=True)]
    pallas_call x1, Pallas kernels: 39.7 us -> 49.1 us  [factor_inverse(): pl.pallas_call(lambda *refs: factor_inverse_kernel(k // B, *refs), out_sh...]
    all_to_all x1 -> x0, starting transfers between devices: 4.61 us -> none  [body(): lax.all_to_all(right, 'blk', split_axis=1, concat_axis=0, tiled=True)]
    ppermute x6 -> x0, waiting for transfers between devices: 4.41 us -> none  [the longest x3 4.41 us: body(): high = lambda x: lax.ppermute(x, 'grp', down)]
  transfers between devices with their start and end apart: 10 -> 1, of which waited for: 6 -> 0; matrix products, arithmetic and copies ran while one was open for 8% -> 4% of each run, Pallas kernels for 16% -> 30%
where the time goes in v2:
time: 162 us; the launch traced here: 161 us
  Pallas kernels  120 us (74%)
  between operations  15.6 us (10%)
  matrix products  12.1 us (7%)
  local copies, waits for them, and re-layouts  11.4 us (7%)
  other arithmetic  1.71 us (1%)
    pallas_call x1, Pallas kernels, gather_sketched(): pl.pallas_call(gather_kernel, out_shape=(jax.ShapeDtypeStruct((blks, rows...  71.4 us
    pallas_call x1, Pallas kernels, factor_inverse(): pl.pallas_call(lambda *refs: factor_inverse_kernel(k // B, *refs), out_sh...  49.1 us
    dot_general x4, matrix products, dot32(): lax.dot_general(a, b, (dims, ((), ())), preferred_element_type=jnp.float3...  12.1 us
    unnamed x11, local copies, waits for them, and re-layouts  3.78 us
  transfers between devices with their start and end apart: 1, of which 0 were waited for; matrix products, arithmetic and copies ran while one was open for 4% of the time, Pallas kernels for 30%

profile of v2, /device:TPU:0, one launch (start us, length us, event | category | flops | bytes accessed | tf_op | source)
XLA Modules:
  0.0 161.3 jit_solution(889948914381272940)
XLA Ops:
  7.2 0.0 copy-start.2
  7.2 0.0 copy-start.1
  7.2 0.0 copy-start.3
  7.2 0.0 copy-start.4
  7.2 0.0 all-gather.2.cloned.1.call-start
  8.6 1.1 copy.17
  9.8 1.4 reshape_squeeze.3
  11.2 0.1 copy.25
  11.4 0.1 pad_maximum_fusion.pieces
  11.5 0.0 copy-done.3
  11.6 0.0 copy-done.4
  11.6 0.0 copy-done.2
  11.6 0.0 copy-done.1
  11.6 71.4 %shard_map.86 = (bf16[16,192,768]{2,1,0:T(8,128)(2,1)}, bf16[3,16,96,192]{3,2,1,0:T(8,128)(2,1)S(1)}) custom-call(bf16[48,3072]{1,0:T(8,128)(2,1)S(1)} %bitcast.39, bf16[192,768]{1,0:T(8,128)(2,1)S(1)} %bitcast.41, f32[3,3072]{1,0:T(4,128)S(1)} %pad_maximum_fusion.1.gates, bf16[3072,768]{1,0:T(8,128)(2,1)} %sketch_hbm.1, f32[192,1]{1,0:T(8,128)S(1)} %fusion.5.rowm, ...), custom_call_target="tpu_custom_call" | custom-call | tf_op jit(solution)/shard_map/pallas_call | solution.py:359
  83.0 1.3 fusion.7
  84.3 0.4 copy.19
  84.8 1.2 reshape.55
  86.0 3.9 %convolution_convert_fusion = bf16[144,768]{1,0:T(8,128)(2,1)} fusion(bf16[144,3072]{1,0:T(8,128)(2,1)S(1)} %reshape.55, bf16[3072,768]{1,0:T(8,128)(2,1)} %bitcast.37), kind=kOutput, calls=%fused_computation.6 | convolution fusion | flops 679587840 | bytes 5824512 | tf_op jit(solution)/shard_map/dot_general | solution.py:139
  89.9 0.0 all-gather.2.cloned.1.call-update
  89.9 1.5 bitcast_convert_fusion
  91.4 1.9 %copy.18 = f32[3,768,192]{1,2,0:T(8,128)} copy(f32[3,768,192]{2,1,0:T(8,128)S(1)} %bitcast_convert_fusion) | data formatting | bytes 3538944 | tf_op jit(solution)/shard_map/convert_element_type | solution.py:423
  93.3 0.1 constant_dynamic-slice_fusion
  93.4 0.0 copy-start
  93.4 2.3 %copy-done = bf16[16,192,768]{2,1,0:T(8,128)(2,1)S(1)} copy-done((bf16[16,192,768]{2,1,0:T(8,128)(2,1)S(1)}, bf16[16,192,768]{2,1,0:T(8,128)(2,1)}, u32[]{:S(2)}) %copy-start) | copy-done | bytes 4718616
  95.7 49.1 %shard_map.87 = f32[768,768]{1,0:T(8,128)S(1)} custom-call(bf16[3072,768]{1,0:T(8,128)(2,1)S(1)} %bitcast.38, f32[1,768]{1,0:T(1,128)S(1)} %broadcast_subtract_fusion.refs_1_), custom_call_target="tpu_custom_call" | custom-call | flops 20000000000 | bytes 100000000 | tf_op jit(solution)/shard_map/pallas_call | solution.py:126
  144.8 2.3 %fusion.1 = f32[1,192,768]{2,1,0:T(8,128)} fusion(f32[768,768]{1,0:T(8,128)S(1)} %shard_map.87, bf16[16,192,768]{2,1,0:T(8,128)(2,1)S(1)} %copy-done, s32[]{:T(128)S(6)} %select_n.27), kind=kOutput, calls=%fused_computation.5 | convolution fusion | flops 1359101952 | bytes 3244036 | tf_op jit(solution)/shard_map/dot_general | solution.py:139
  147.1 0.0 all-gather.2.cloned.1.call-done
  147.1 3.4 %convolution_bitcast_fusion = f32[192,768]{1,0:T(8,128)S(1)} fusion(bf16[3,768,768]{2,1,0:T(8,128)(2,1)} %all-gather.2.cloned.1.call-done, f32[3,768,192]{1,2,0:T(8,128)} %copy.18, f32[3,192]{1,0:T(4,128)S(1)} %constant_dynamic-slice_fusion), kind=kOutput, calls=%fused_computation.3 | convolution fusion | flops 680361984 | bytes 5900544 | tf_op jit(solution)/shard_map/dot_general | solution.py:139
  150.5 2.5 %fusion = f32[192,1,768]{2,0,1:T(8,128)S(1)} fusion(f32[192,768]{1,0:T(8,128)S(1)} %convolution_bitcast_fusion, f32[768,768]{1,0:T(8,128)S(1)} %shard_map.87), kind=kOutput, calls=%fused_computation.2 | convolution fusion | flops 1359101952 | bytes 3538944 | tf_op jit(solution)/shard_map/dot_general | solution.py:139
  153.0 1.4 copy.20
  (5 shorter events, 0.1 us)
Async XLA Ops:
  7.2 4.5 %copy-start.2 = (bf16[1,192,768]{2,1,0:T(8,128)(2,1)S(1)}, bf16[1,192,768]{2,1,0:T(8,128)(2,1)}, u32[]{:S(2)}) copy-start(bf16[1,192,768]{2,1,0:T(8,128)(2,1)} %param.7) | copy-start | bytes 884740
  7.2 4.5 %copy-start.1 = (bf16[1,48,3072]{2,1,0:T(8,128)(2,1)S(1)}, bf16[1,48,3072]{2,1,0:T(8,128)(2,1)}, u32[]{:S(2)}) copy-start(bf16[1,48,3072]{2,1,0:T(8,128)(2,1)} %param.8) | copy-start | bytes 884740
  7.2 4.3 %copy-start.3 = (f32[1,3072]{1,0:T(1,128)S(1)}, f32[1,3072]{1,0:T(1,128)}, u32[]{:S(2)}) copy-start(f32[1,3072]{1,0:T(1,128)} %param.10) | copy-start | bytes 36868
  7.2 4.4 %copy-start.4 = (f32[1,3072]{1,0:T(1,128)S(1)}, f32[1,3072]{1,0:T(1,128)}, u32[]{:S(2)}) copy-start(f32[1,3072]{1,0:T(1,128)} %param.9) | copy-start | bytes 36868
  7.2 139.9 %all-gather.2.cloned.1.call-start = ((), (), s32[]{:S(2)}) async-start(), calls=%async_computation | async-start | bytes 3760128 | tf_op jit(solution)/shard_map/all_gather | solution.py:418
  93.4 2.3 %copy-start = (bf16[16,192,768]{2,1,0:T(8,128)(2,1)S(1)}, bf16[16,192,768]{2,1,0:T(8,128)(2,1)}, u32[]{:S(2)}) copy-start(bf16[16,192,768]{2,1,0:T(8,128)(2,1)} %get-tuple-element.4) | copy-start | bytes 14155780
Sparse Core Ops, SparseCore 0:
  90.0 50.2 all-gather.1

commit v3 on v1

v3 whole, which is shorter than its diff:
```python
import math

import jax
import jax.numpy as jnp
from jax import lax
from jax.experimental import pallas as pl
from jax.experimental.pallas import tpu as pltpu
from jax.sharding import PartitionSpec as P

HIGH = lax.Precision.HIGHEST
B = 128
W = 2 * B
SIDE = 4
BLKS = SIDE * SIDE
MESH = pl.DeviceIdType.MESH


def pivot_inverse(a, hooks):
    lane = lax.broadcasted_iota(jnp.int32, (8, B), 1)
    sub = lax.broadcasted_iota(jnp.int32, (8, B), 0)
    n = B // 8
    rest = a.reshape(n, 8, B)
    out = []
    wide = lambda x: jnp.broadcast_to(x, (8, B))
    for q in range(n):
        k = 8 * q
        slab = rest[0]
        cols = [wide(slab[:, k + t : k + t + 1]) for t in range(8)]
        piv = [[wide(cols[j][i : i + 1, :]) if j <= i else None for j in range(8)] for i in range(8)]
        inside = (lane >= k) & (lane < k + 8)
        e = [
            jnp.where(lane == k + t, 1.0, jnp.where(inside, 0.0, wide(slab[t : t + 1, :])))
            for t in range(8)
        ]
        fin, s, u, ds = [None] * 8, [None] * 8, {}, []
        for t in range(0, 8, 2):
            p0, p1, p2 = piv[t][t], piv[t + 1][t], piv[t + 1][t + 1]
            det = p0 * p2 - p1 * p1
            rd = pl.reciprocal(det, approx=True)
            rd = rd * (2.0 - det * rd)
            i0, i1, i2 = p2 * rd, p1 * rd, p0 * rd
            ds.append((i0, i1, i2))
            for i in range(t + 2, 8):
                x0, x1 = piv[i][t], piv[i][t + 1]
                u[i, t] = x0 * i0 - x1 * i1
                u[i, t + 1] = x1 * i2 - x0 * i1
            for i in range(t + 2, 8):
                for j in range(t + 2, i + 1):
                    piv[i][j] = piv[i][j] - (u[i, t] * piv[j][t] + u[i, t + 1] * piv[j][t + 1])
                e[i] = e[i] - (u[i, t] * e[t] + u[i, t + 1] * e[t + 1])
            ra = lax.rsqrt(p0)
            m = p1 * ra * ra
            fin[t] = e[t] * ra
            fin[t + 1] = (e[t + 1] - m * e[t]) * lax.rsqrt(p2 - m * p1)
        if q < n - 1:
            for t in range(6, -1, -2):
                i0, i1, i2 = ds[t // 2]
                v0 = e[t] * i0 - e[t + 1] * i1
                v1 = e[t + 1] * i2 - e[t] * i1
                for i in range(7, t + 1, -1):
                    v0 = v0 - u[i, t] * s[i]
                    v1 = v1 - u[i, t + 1] * s[i]
                s[t], s[t + 1] = v0, v1
            rest = rest[1:]
            new = jnp.where(inside[None], 0.0, rest)
            for t in range(8):
                new = new - jnp.broadcast_to(rest[:, :, k + t : k + t + 1], rest.shape) * s[t][None]
            rest = new
        o = fin[0]
        for t in range(1, 8):
            o = jnp.where(sub == t, fin[t], o)
        out.append(jnp.where(lane <= sub + k, o, 0.0))
        if q in hooks:
            hooks[q]()
    return jnp.concatenate(out, axis=0)


def remote(src, dst, send, recv, to):
    return pltpu.make_async_remote_copy(
        src_ref=src, dst_ref=dst, send_sem=send, recv_sem=recv, device_id=to, device_id_type=MESH
    )


class Ring:
    def __init__(self, buf, split, send, recv, cx, cy, me):
        self.buf, self.split, self.send, self.recv = buf, split, send, recv
        self.cx, self.cy, self.me = cx, cy, me
        self.half_of = {}

    def view(self, c, owner, half):
        rows = self.buf.shape[2]
        at = pl.ds(0, self.split) if half == 0 else pl.ds(self.split, rows - self.split)
        return self.buf.at[c, owner, at, :]

    def owner(self, half, r1, r2):
        c1, c2 = (self.cx, self.cy) if half == 0 else (self.cy, self.cx)
        a, b = lax.rem(c1 + r1, SIDE), lax.rem(c2 + r2, SIDE)
        return a * SIDE + b if half == 0 else b * SIDE + a

    def ship(self, c, half, block, axis, step):
        to = self.owner(half, step, 0) if axis == 0 else self.owner(half, 0, step)
        ref = self.view(c, block, half)
        n = self.count
        self.count += 1
        self.half_of[n] = half
        remote(ref, ref, self.send.at[c, n], self.recv.at[c, half, block], {"blk": to}).start()

    def take(self, c, half, r1, r2):
        block = self.owner(half, r1, r2)
        ref = self.view(c, block, half)
        other = {"blk": lax.rem(self.me + 1, BLKS)}
        remote(ref, ref, self.send.at[c, 0], self.recv.at[c, half, block], other).wait_recv()
        return block

    def relay(self, c, half, r1):
        low = self.take(c, half, r1, 3)
        if r1 in (0, 3):
            self.ship(c, half, low, 1, 1)
        high = self.take(c, half, r1, 1)
        if r1 in (1, 2):
            self.ship(c, half, high, 1, 3)

    def spread(self, c, half, block):
        self.ship(c, half, block, 1, 1)
        self.ship(c, half, block, 1, 3)

    def stage(self, c, k):
        if k == 0:
            self.count = 0
            for half in range(2):
                self.ship(c, half, self.me, 0, 1)
                self.ship(c, half, self.me, 0, 3)
            for half in range(2):
                self.spread(c, half, self.me)
        elif k == 1:
            self.count = 8
            for half in range(2):
                b = self.take(c, half, 3, 0)
                if half == 0:
                    self.ship(c, half, b, 0, 1)
                self.spread(c, half, b)
                b = self.take(c, half, 1, 0)
                if half == 1:
                    self.ship(c, half, b, 0, 3)
                self.spread(c, half, b)
            for half in range(2):
                self.relay(c, half, 0)
        elif k == 2:
            self.count = 20
            for half in range(2):
                self.spread(c, half, self.take(c, half, 2, 0))
            for half in range(2):
                self.relay(c, half, 3)
                self.relay(c, half, 1)
        elif k == 3:
            self.count = 28
            for half in range(2):
                self.relay(c, half, 2)
        else:
            for half in range(2):
                for r1 in (0, 3, 1, 2):
                    self.take(c, half, r1, 2)

    def drain(self, c):
        other = {"blk": lax.rem(self.me + 1, BLKS)}
        for n in range(30):
            ref = self.view(c, self.me, self.half_of[n])
            remote(ref, ref, self.send.at[c, n], self.recv.at[c, 0, 0], other).wait_send()


def dot(a, b, ca, cb, **kw):
    return lax.dot_general(
        a, b, (((ca,), (cb,)), ((), ())), preferred_element_type=jnp.float32, **kw
    )


def bond_kernel(
    right, left, gates, sketch_hbm, rowm, colm,
    inverse, projected, own_out,
    sketch, stack, mapped, sk, sk_t, joint, right_n, left_n, pieces, got, gates_c, left_t, right_t,
    xcol,
    load_sem, keep_sem, x_send, x_recv, m_send, m_recv, s_send, s_recv, j_send, j_recv,
    a_send, a_recv, n_send, n_recv,
):
    bf16, f32 = jnp.bfloat16, jnp.float32
    g = lax.axis_index("grp")
    me = lax.axis_index("blk")
    groups = lax.axis_size("grp")
    depth, columns = right.shape
    rows, middle = left.shape
    chunks = sk.shape[0]
    total = rows * BLKS
    cols_here = columns // BLKS
    up = {"grp": lax.rem(g + 1, groups)}
    down = {"grp": lax.rem(g + groups - 1, groups)}

    load = pltpu.make_async_copy(sketch_hbm, sketch, load_sem)
    load.start()
    barrier = pltpu.get_barrier_semaphore()
    for peer in [{"blk": lax.rem(me + i, BLKS)} for i in range(1, BLKS)] + [up, down]:
        pl.semaphore_signal(barrier, inc=1, device_id=peer, device_id_type=MESH)
    pl.semaphore_wait(barrier, BLKS + 1)

    started = []

    def go(copy):
        copy.start()
        started.append(copy)

    def x_wait(ref, k):
        remote(ref, ref, x_send.at[k], x_recv.at[k], up).wait_recv()

    for slot, to in ((0, up), (1, down)):
        go(remote(right, right_n.at[slot], x_send.at[slot], x_recv.at[slot], to))
    for slot, to in ((0, up), (1, down)):
        go(remote(left, left_n.at[slot], x_send.at[2 + slot], x_recv.at[2 + slot], to))

    turned = left[...].astype(f32).T.astype(bf16).reshape(BLKS, depth, rows)
    for o in range(BLKS):
        pieces[o, 0:depth, :] = right[:, o * cols_here : (o + 1) * cols_here]
        pieces[o, depth : 2 * depth, :] = turned[o]
        gates_c[o] = gates[:, o * cols_here : (o + 1) * cols_here]
    for i in range(1, BLKS):
        to = lax.rem(me + i, BLKS)
        go(remote(pieces.at[to], got.at[0, me], a_send.at[i], a_recv.at[me], {"blk": to}))
    keep = pltpu.make_async_copy(pieces.at[me], got.at[0, me], keep_sem)
    keep.start()

    cx, cy = me // SIDE, me % SIDE
    ring_m = Ring(mapped, 80, m_send, m_recv, cx, cy, me)
    ring_s = Ring(sk, rows // 2, s_send, s_recv, cx, cy, me)
    ring_j = Ring(joint, 80, j_send, j_recv, cx, cy, me)

    def at(c):
        return slice(c * W, (c + 1) * W)

    def make_mapped(c):
        return dot(stack[...], sketch[:, at(c)], 1, 0).astype(bf16)

    def part(buf, c, t):
        return buf[c, :, t * depth : (t + 1) * depth, :].reshape(BLKS * depth, W)

    def make_sketched(c):
        add = dot(left[...], part(mapped, c, 0), 1, 0)
        add = add + dot(left_n[0], part(mapped, c, 1), 1, 0)
        add = add + dot(left_n[1], part(mapped, c, 2), 1, 0)
        return (add * rowm[...] * colm[c]).astype(bf16)

    def make_joint(c):
        return dot(left_t[...], sk[c].reshape(total, W), 1, 0).astype(bf16)

    def project(c):
        add = dot(right_t[0], part(joint, c, 0), 1, 0)
        add = add + dot(right_t[1], part(joint, c, 1), 1, 0)
        projected[:, at(c)] = add + dot(right_t[2], part(joint, c, 2), 1, 0)

    load.wait()
    stack[0:depth, :] = (right[...].astype(f32) * gates[0:1, :]).astype(bf16)
    for slot in range(2):
        x_wait(right_n.at[slot], slot)
        stack[(slot + 1) * depth : (slot + 2) * depth, :] = (
            right_n[slot].astype(f32) * gates[slot + 1 : slot + 2, :]
        ).astype(bf16)

    def start_mapped(c):
        mapped[c, me] = make_mapped(c)
        ring_m.stage(c, 0)

    def start_sketched(c):
        sk[c, me] = make_sketched(c)
        ring_s.stage(c, 0)

    def advance(ring, *pairs):
        for c, k in pairs:
            ring.stage(c, k)

    def pieces_in():
        keep.wait()
        for i in range(1, BLKS):
            o = lax.rem(me + i, BLKS)
            ref = got.at[0, o]
            remote(ref, ref, a_send.at[i], a_recv.at[o], {"blk": o}).wait_recv()
        for slot, to in ((0, up), (1, down)):
            go(remote(got.at[0], got.at[1 + slot], n_send.at[slot], n_recv.at[slot], to))

    def pieces_done():
        for slot in range(2):
            ref = got.at[1 + slot]
            remote(ref, ref, n_send.at[slot], n_recv.at[slot], up).wait_recv()
        mine = gates_c[me]
        for t in range(3):
            both = got[t]
            scaled = both[:, :depth].reshape(middle, cols_here).astype(f32) * mine[t : t + 1, :]
            right_t[t] = scaled.T.astype(bf16)
            for o in range(0, BLKS, 2):
                left_t[t * depth : (t + 1) * depth, o * rows : (o + 2) * rows] = jnp.concatenate(
                    [both[o, depth:], both[o + 1, depth:]], axis=1
                )

    start_mapped(0)
    start_mapped(1)
    advance(ring_m, (0, 1))
    start_mapped(2)
    advance(ring_m, (1, 1))
    advance(ring_m, (0, 2), (1, 2), (2, 1))
    pieces_in()
    advance(ring_m, (0, 3), (1, 3), (2, 2))
    for slot in range(2):
        x_wait(left_n.at[slot], 2 + slot)
    advance(ring_m, (0, 4))
    start_sketched(0)
    advance(ring_m, (1, 4), (2, 3))
    start_sketched(1)
    advance(ring_s, (0, 1))
    inverse[...] = jnp.zeros_like(inverse)
    advance(ring_m, (2, 4))
    advance(ring_s, (0, 2), (1, 1))
    start_sketched(2)
    pieces_done()
    advance(ring_s, (0, 3), (1, 2), (2, 1))

    def start_joint(c):
        joint[c, me] = make_joint(c)
        ring_j.stage(c, 0)

    def finish_joint(c):
        ring_j.stage(c, 4)
        project(c)

    M, S, J = (lambda c, k, r=r: (r.stage, c, k) for r in (ring_m, ring_s, ring_j))
    even = {
        0: [S(0, 4), S(1, 3), S(2, 2)],
        1: [S(2, 4), J(0, 1)],
        2: [J(0, 3), J(1, 1), (start_joint, 2)],
        3: [J(1, 3), J(2, 2)],
        4: [(finish_joint, 2)],
    }
    odd = {
        0: [S(1, 4), S(2, 3), (start_joint, 0)],
        1: [(start_joint, 1), J(0, 2)],
        2: [(finish_joint, 0), J(1, 2), J(2, 1)],
        3: [(finish_joint, 1), J(2, 3)],
    }

    def run(c, table):
        for cc, todo in table.items():

            @pl.when(c == cc)
            def _(todo=todo):
                for f, *args in todo:
                    f(*args)

    eye = lax.broadcasted_iota(jnp.int32, (B, B), 0) == lax.broadcasted_iota(jnp.int32, (B, B), 1)

    blocks = chunks * (W // B)

    def step(c, carry):
        here = pl.multiple_of(c * B, B)
        ch = c // 2
        off = pl.multiple_of((c % 2) * B, B)
        run(c, even)

        @pl.when(c % 2 == 0)
        def _():
            sk_t[pl.ds(here, W), :] = sk[ch].reshape(total, W).astype(f32).T.astype(bf16)

            def gram(i, cc):
                ii = pl.multiple_of(i * W, W)
                xcol[pl.ds(ii, W), :] = dot(sk_t[pl.ds(ii, W), :], sk[ch].reshape(total, W), 1, 0)
                return cc

            lax.fori_loop(0, ch + 1, gram, 0)

        for cc in range(1, blocks):

            @pl.when(c == cc)
            def _(k=cc * B, mine=slice((cc % 2) * B, (cc % 2 + 1) * B)):
                x = dot(inverse[0:k, 0:k], xcol[0:k, mine], 1, 0, precision=HIGH)
                xt = x.T
                xcol[k : k + B, mine] = xcol[k : k + B, mine] - dot(xt, x, 1, 0, precision=HIGH)
                inverse[k : k + B, 0:k] = dot(xt, inverse[0:k, 0:k], 1, 0, precision=HIGH)

        a = xcol[pl.ds(here, B), pl.ds(off, B)] + jnp.where(eye, 1.0 - colm[ch, :, pl.ds(off, B)], 0.0)
        inv = pivot_inverse(a, {9: lambda: run(c, odd)})
        for cc in range(1, blocks):

            @pl.when(c == cc)
            def _(k=cc * B):
                inverse[k : k + B, 0:k] = -dot(inv, inverse[k : k + B, 0:k], 1, 0, precision=HIGH)

        inverse[pl.ds(here, B), pl.ds(here, B)] = inv
        return carry

    lax.fori_loop(0, blocks, step, 0)
    for c in range(chunks):
        own_out[:, c * W : (c + 1) * W] = sk[c, me]

    def drain(c, carry):
        ring_m.drain(c)
        ring_s.drain(c)
        ring_j.drain(c)
        return carry

    lax.fori_loop(0, chunks, drain, 0)
    for copy in started:
        copy.wait_send()


def bond(right, left, gates, sketch, rowm, colm):
    bf16, f32 = jnp.bfloat16, jnp.float32
    rows, middle = left.shape
    depth, columns = right.shape
    width = sketch.shape[1]
    chunks = width // W
    cols_here = columns // BLKS
    vmem = pl.BlockSpec(memory_space=pltpu.VMEM)
    dma = pltpu.SemaphoreType.DMA
    return pl.pallas_call(
        bond_kernel,
        out_shape=(
            jax.ShapeDtypeStruct((width, width), f32),
            jax.ShapeDtypeStruct((cols_here, width), f32),
            jax.ShapeDtypeStruct((rows, width), bf16),
        ),
        in_specs=[vmem, vmem, vmem, pl.BlockSpec(memory_space=pl.ANY), vmem, vmem],
        out_specs=(vmem, vmem, vmem),
        scratch_shapes=[
            pltpu.VMEM((columns, width), bf16),
            pltpu.VMEM((3 * depth, columns), bf16),
            pltpu.VMEM((chunks, BLKS, 3 * depth, W), bf16),
            pltpu.VMEM((chunks, BLKS, rows, W), bf16),
            pltpu.VMEM((width, rows * BLKS), bf16),
            pltpu.VMEM((chunks, BLKS, 3 * depth, W), bf16),
            pltpu.VMEM((2, depth, columns), bf16),
            pltpu.VMEM((2, rows, middle), bf16),
            pltpu.VMEM((BLKS, 2 * depth, rows), bf16),
            pltpu.VMEM((3, BLKS, 2 * depth, rows), bf16),
            pltpu.VMEM((BLKS, 3, cols_here), f32),
            pltpu.VMEM((3 * depth, rows * BLKS), bf16),
            pltpu.VMEM((3, cols_here, middle), bf16),
            pltpu.VMEM((width, W), f32),
            dma(()),
            dma(()),
            dma((4,)),
            dma((4,)),
            dma((chunks, 30)),
            dma((chunks, 2, BLKS)),
            dma((chunks, 30)),
            dma((chunks, 2, BLKS)),
            dma((chunks, 30)),
            dma((chunks, 2, BLKS)),
            dma((BLKS,)),
            dma((BLKS,)),
            dma((2,)),
            dma((2,)),
        ],
        compiler_params=pltpu.CompilerParams(
            collective_id=0, has_side_effects=True, vmem_limit_bytes=50 * 2**20
        ),
    )(right, left, gates, sketch, rowm, colm)


def dot32(a, b, dims, **kw):
    return lax.dot_general(a, b, (dims, ((), ())), preferred_element_type=jnp.float32, **kw)


def body(left_tensor, right_tensor, diag_gate, hop_gate, sketch, sector_rows, kept):
    f32 = jnp.float32
    left, right, diag, hop = left_tensor[0], right_tensor[0], diag_gate[0], hop_gate[0]
    rows_here, middle = left.shape
    width = sketch.shape[1]
    total = rows_here * lax.axis_size("blk")
    g, me = lax.axis_index("grp"), lax.axis_index("blk")
    hop_low = jnp.where(g > 0, hop, 0.0)
    hop_high = jnp.where(g < lax.axis_size("grp") - 1, hop, 0.0)
    gates = jnp.stack([diag, hop_low, hop_high])
    row_index = me * rows_here + jnp.arange(rows_here, dtype=jnp.int32)
    rowm = (row_index[:, None] < sector_rows[0]).astype(f32)
    colm = (jnp.arange(width, dtype=jnp.int32).reshape(-1, 1, W) < kept[0]).astype(f32)
    inverse, projected, sketched = bond(right, left, gates, sketch, rowm, colm)
    scale = math.sqrt(total)
    left_out = dot32(sketched.astype(f32), inverse, ((1,), (1,)), precision=HIGH) * scale
    right_out = dot32(projected, inverse, ((1,), (1,)), precision=HIGH) / scale
    return (left_out[None], right_out[:, None, :])


def solution(mesh):
    in_specs = (
        P("grp", "blk", None),
        P("grp", "blk", None),
        P("grp", None),
        P("grp", None),
        P(),
        P("grp"),
        P("grp"),
    )
    out_specs = (P("grp", "blk", None), P("blk", "grp", None))
    return jax.shard_map(body, mesh=mesh, in_specs=in_specs, out_specs=out_specs, check_vma=False)
```

time: 253 us -> 134 us (0.53)
  waiting for transfers between devices: 145 us -> 0 us
  Pallas kernels: 39.7 us -> 122 us
  matrix products: 26.8 us -> 4.76 us
  starting transfers between devices: 18.9 us -> 0 us
  between operations: 15.3 us -> 1.98 us
    all_gather x3 -> x0, waiting for transfers between devices: 130 us -> none  [the longest x1 49.1 us: body(): sketched_all = lax.all_gather(sketched, 'blk', axis=0, tiled=True)]
    pallas_call x1, Pallas kernels: 39.7 us -> 122 us  [bond(): pl.pallas_call(bond_kernel, out_shape=(jax.ShapeDtypeStruct((width, width...]
    dot_general x7 -> x2, matrix products: 26.8 us -> 4.76 us  [dot32(): lax.dot_general(a, b, (dims, ((), ())), preferred_element_type=jnp.float3...]
    ppermute x6 -> x0, starting transfers between devices: 14.2 us -> none  [the longest x3 10.1 us: body(): low = lambda x: lax.ppermute(x, 'grp', up)]
    all_to_all x1 -> x0, waiting for transfers between devices: 10.6 us -> none  [body(): lax.all_to_all(right, 'blk', split_axis=1, concat_axis=0, tiled=True)]
    all_to_all x1 -> x0, starting transfers between devices: 4.61 us -> none  [body(): lax.all_to_all(right, 'blk', split_axis=1, concat_axis=0, tiled=True)]
    ppermute x6 -> x0, waiting for transfers between devices: 4.41 us -> none  [the longest x3 4.41 us: body(): high = lambda x: lax.ppermute(x, 'grp', down)]
  transfers between devices with their start and end apart: 10 -> 0, of which waited for: 6 -> 0; matrix products, arithmetic and copies ran while one was open for 8% -> 0% of each run, Pallas kernels for 16% -> 0%
where the time goes in v3:
time: 134 us; the launch traced here: 133 us
  Pallas kernels  122 us (91%)
  matrix products  4.76 us (4%)
  local copies, waits for them, and re-layouts  3.34 us (2%)
  between operations  1.98 us (1%)
  other arithmetic  1.5 us (1%)
    pallas_call x1, Pallas kernels, bond(): pl.pallas_call(bond_kernel, out_shape=(jax.ShapeDtypeStruct((width, width...  122 us
    dot_general x2, matrix products, dot32(): lax.dot_general(a, b, (dims, ((), ())), preferred_element_type=jnp.float3...  4.76 us
    unnamed x5, local copies, waits for them, and re-layouts  3.34 us

profile of v3, /device:TPU:0, one launch (start us, length us, event | category | flops | bytes accessed | tf_op | source)
XLA Modules:
  0.0 133.3 jit_solution(12494433333050719589)
XLA Ops:
  0.6 0.7 broadcast_select_fusion.1
  1.4 0.7 pad_maximum_fusion.gates
  3.5 0.0 copy-start
  3.5 1.0 copy-done
  4.4 0.0 copy-start.1
  4.4 1.0 copy-done.1
  5.4 121.7 %shard_map.86 = (f32[768,768]{1,0:T(8,128)S(1)}, f32[192,768]{1,0:T(8,128)S(1)}, bf16[192,768]{1,0:T(8,128)(2,1)S(1)}) custom-call(bf16[48,3072]{1,0:T(8,128)(2,1)S(1)} %bitcast.14, bf16[192,768]{1,0:T(8,128)(2,1)S(1)} %bitcast.15, f32[3,3072]{1,0:T(4,128)S(1)} %pad_maximum_fusion.gates, bf16[3072,768]{1,0:T(8,128)(2,1)} %sketch_hbm.1, ...), custom_call_target="tpu_custom_call" | custom-call | tf_op jit(solution)/shard_map/pallas_call | solution.py:418
  127.1 2.5 %fusion = f32[192,1,768]{2,0,1:T(8,128)S(1)} fusion(f32[192,768]{1,0:T(8,128)S(1)} %get-tuple-element.7, f32[768,768]{1,0:T(8,128)S(1)} %get-tuple-element.6), kind=kOutput, calls=%fused_computation.1 | convolution fusion | flops 1359101952 | bytes 3538944 | tf_op jit(solution)/shard_map/dot_general | solution.py:464
  129.6 1.4 %copy.11 = f32[192,1,768]{2,1,0:T(1,128)} copy(f32[192,1,768]{2,0,1:T(8,128)S(1)} %fusion) | data formatting | bytes 1179648
  131.0 2.3 %fusion.1 = f32[1,192,768]{2,1,0:T(8,128)} fusion(bf16[192,768]{1,0:T(8,128)(2,1)S(1)} %get-tuple-element.5, f32[768,768]{1,0:T(8,128)S(1)} %get-tuple-element.6), kind=kOutput, calls=%fused_computation.3 | convolution fusion | flops 1359101952 | bytes 3244032 | tf_op jit(solution)/shard_map/dot_general | solution.py:464
  (2 shorter events, 0.0 us)
Async XLA Ops:
  3.5 1.0 copy-start
  4.4 1.0 copy-start.1

commit v4 on v3

--- a/solution.py
+++ b/solution.py
@@ -9,7 +9,7 @@
 
 HIGH = lax.Precision.HIGHEST
 B = 128
-W = 2 * B
+WIDTHS = (B, 2 * B, 3 * B)
 SIDE = 4
 BLKS = SIDE * SIDE
 MESH = pl.DeviceIdType.MESH
@@ -88,9 +88,9 @@
         self.half_of = {}
 
     def view(self, c, owner, half):
-        rows = self.buf.shape[2]
+        rows = self.buf[c].shape[1]
         at = pl.ds(0, self.split) if half == 0 else pl.ds(self.split, rows - self.split)
-        return self.buf.at[c, owner, at, :]
+        return self.buf[c].at[owner, at, :]
 
     def owner(self, half, r1, r2):
         c1, c2 = (self.cx, self.cy) if half == 0 else (self.cy, self.cx)
@@ -161,6 +161,24 @@
                 for r1 in (0, 3, 1, 2):
                     self.take(c, half, r1, 2)
 
+    def direct(self, c):
+        ref = self.buf[c].at[self.me]
+        for i in range(1, BLKS):
+            to = lax.rem(self.me + i, BLKS)
+            remote(ref, ref, self.send.at[c, i], self.recv.at[c, 0, self.me], {"blk": to}).start()
+
+    def direct_done(self, c):
+        for i in range(1, BLKS):
+            o = lax.rem(self.me + i, BLKS)
+            ref = self.buf[c].at[o]
+            remote(ref, ref, self.send.at[c, i], self.recv.at[c, 0, o], {"blk": o}).wait_recv()
+
+    def direct_drain(self, c):
+        ref = self.buf[c].at[self.me]
+        for i in range(1, BLKS):
+            o = lax.rem(self.me + i, BLKS)
+            remote(ref, ref, self.send.at[c, i], self.recv.at[c, 0, o], {"blk": o}).wait_send()
+
     def drain(self, c):
         other = {"blk": lax.rem(self.me + 1, BLKS)}
         for n in range(30):
@@ -168,6 +186,14 @@
             remote(ref, ref, self.send.at[c, n], self.recv.at[c, 0, 0], other).wait_send()
 
 
+def dot3(a, b):
+    f32, bf16 = jnp.float32, jnp.bfloat16
+    ah, bh = a.astype(bf16), b.astype(bf16)
+    al = (a - ah.astype(f32)).astype(bf16)
+    bl = (b - bh.astype(f32)).astype(bf16)
+    return dot(ah, bh, 1, 0) + (dot(ah, bl, 1, 0) + dot(al, bh, 1, 0))
+
+
 def dot(a, b, ca, cb, **kw):
     return lax.dot_general(
         a, b, (((ca,), (cb,)), ((), ())), preferred_element_type=jnp.float32, **kw
@@ -175,11 +201,11 @@
 
 
 def bond_kernel(
-    right, left, gates, sketch_hbm, rowm, colm,
+    right_hbm, left_hbm, diag_hbm, hop_hbm, sketch_hbm, live_rows, kept,
     inverse, projected, own_out,
-    sketch, stack, mapped, sk, sk_t, joint, right_n, left_n, pieces, got, gates_c, left_t, right_t,
+    right, left, hop, gates, rowm, colm, sketch, stack, m0, m1, m2, k0, k1, k2, sk_t, j0, j1, j2, right_n, left_n, pieces, got, gates_c, left_t, right_t,
     xcol,
-    load_sem, keep_sem, x_send, x_recv, m_send, m_recv, s_send, s_recv, j_send, j_recv,
+    load_sem, right_sem, left_sem, diag_sem, hop_sem, keep_sem, x_send, x_recv, m_send, m_recv, s_send, s_recv, j_send, j_recv,
     a_send, a_recv, n_send, n_recv,
 ):
     bf16, f32 = jnp.bfloat16, jnp.float32
@@ -188,17 +214,36 @@
     groups = lax.axis_size("grp")
     depth, columns = right.shape
     rows, middle = left.shape
-    chunks = sk.shape[0]
+    mapped, sk, joint = (m0, m1, m2), (k0, k1, k2), (j0, j1, j2)
+    starts = [sum(WIDTHS[:c]) for c in range(len(WIDTHS))]
     total = rows * BLKS
     cols_here = columns // BLKS
     up = {"grp": lax.rem(g + 1, groups)}
     down = {"grp": lax.rem(g + groups - 1, groups)}
 
     load = pltpu.make_async_copy(sketch_hbm, sketch, load_sem)
+    load_right = pltpu.make_async_copy(right_hbm, right, right_sem)
+    load_left = pltpu.make_async_copy(left_hbm, left, left_sem)
+    load_right.start()
+    load_left.start()
+    load_diag = pltpu.make_async_copy(diag_hbm, gates.at[pl.ds(0, 1)], diag_sem)
+    load_hop = pltpu.make_async_copy(hop_hbm, hop, hop_sem)
+    load_diag.start()
+    load_hop.start()
     load.start()
     barrier = pltpu.get_barrier_semaphore()
     for peer in [{"blk": lax.rem(me + i, BLKS)} for i in range(1, BLKS)] + [up, down]:
         pl.semaphore_signal(barrier, inc=1, device_id=peer, device_id_type=MESH)
+    load_diag.wait()
+    load_hop.wait()
+    gates[1:2, :] = jnp.where(g > 0, hop[...], 0.0)
+    gates[2:3, :] = jnp.where(g < groups - 1, hop[...], 0.0)
+    row = me * rows + lax.broadcasted_iota(jnp.int32, (rows, 1), 0)
+    rowm[...] = jnp.where(row < live_rows[0], 1.0, 0.0)
+    col = lax.broadcasted_iota(jnp.int32, colm.shape, 1)
+    colm[...] = jnp.where(col < kept[0], 1.0, 0.0)
+    load_right.wait()
+    load_left.wait()
     pl.semaphore_wait(barrier, BLKS + 1)
 
     started = []
@@ -217,8 +262,9 @@
 
     turned = left[...].astype(f32).T.astype(bf16).reshape(BLKS, depth, rows)
     for o in range(BLKS):
-        pieces[o, 0:depth, :] = right[:, o * cols_here : (o + 1) * cols_here]
-        pieces[o, depth : 2 * depth, :] = turned[o]
+        pieces[o] = jnp.concatenate(
+            [right[:, o * cols_here : (o + 1) * cols_here], turned[o]], axis=1
+        )
         gates_c[o] = gates[:, o * cols_here : (o + 1) * cols_here]
     for i in range(1, BLKS):
         to = lax.rem(me + i, BLKS)
@@ -232,22 +278,22 @@
     ring_j = Ring(joint, 80, j_send, j_recv, cx, cy, me)
 
     def at(c):
-        return slice(c * W, (c + 1) * W)
+        return slice(starts[c], starts[c] + WIDTHS[c])
 
     def make_mapped(c):
         return dot(stack[...], sketch[:, at(c)], 1, 0).astype(bf16)
 
     def part(buf, c, t):
-        return buf[c, :, t * depth : (t + 1) * depth, :].reshape(BLKS * depth, W)
+        return buf[c][:, t * depth : (t + 1) * depth, :].reshape(BLKS * depth, WIDTHS[c])
 
     def make_sketched(c):
         add = dot(left[...], part(mapped, c, 0), 1, 0)
         add = add + dot(left_n[0], part(mapped, c, 1), 1, 0)
         add = add + dot(left_n[1], part(mapped, c, 2), 1, 0)
-        return (add * rowm[...] * colm[c]).astype(bf16)
+        return (add * rowm[...] * colm[:, at(c)]).astype(bf16)
 
     def make_joint(c):
-        return dot(left_t[...], sk[c].reshape(total, W), 1, 0).astype(bf16)
+        return dot(left_t[...], sk[c][...].reshape(total, WIDTHS[c]), 1, 0).astype(bf16)
 
     def project(c):
         add = dot(right_t[0], part(joint, c, 0), 1, 0)
@@ -263,12 +309,18 @@
         ).astype(bf16)
 
     def start_mapped(c):
-        mapped[c, me] = make_mapped(c)
-        ring_m.stage(c, 0)
+        mapped[c][me] = make_mapped(c)
+        if c:
+            ring_m.stage(c, 0)
+        else:
+            ring_m.direct(c)
 
     def start_sketched(c):
-        sk[c, me] = make_sketched(c)
-        ring_s.stage(c, 0)
+        sk[c][me] = make_sketched(c)
+        if c:
+            ring_s.stage(c, 0)
+        else:
+            ring_s.direct(c)
 
     def advance(ring, *pairs):
         for c, k in pairs:
@@ -290,57 +342,64 @@
         mine = gates_c[me]
         for t in range(3):
             both = got[t]
-            scaled = both[:, :depth].reshape(middle, cols_here).astype(f32) * mine[t : t + 1, :]
+            scaled = both[:, :, :cols_here].reshape(middle, cols_here).astype(f32) * mine[t : t + 1, :]
             right_t[t] = scaled.T.astype(bf16)
             for o in range(0, BLKS, 2):
                 left_t[t * depth : (t + 1) * depth, o * rows : (o + 2) * rows] = jnp.concatenate(
-                    [both[o, depth:], both[o + 1, depth:]], axis=1
+                    [both[o, :, cols_here:], both[o + 1, :, cols_here:]], axis=1
                 )
 
     start_mapped(0)
     start_mapped(1)
-    advance(ring_m, (0, 1))
+    advance(ring_m, (1, 1))
     start_mapped(2)
-    advance(ring_m, (1, 1))
-    advance(ring_m, (0, 2), (1, 2), (2, 1))
-    pieces_in()
-    advance(ring_m, (0, 3), (1, 3), (2, 2))
+    ring_m.direct_done(0)
     for slot in range(2):
         x_wait(left_n.at[slot], 2 + slot)
-    advance(ring_m, (0, 4))
     start_sketched(0)
-    advance(ring_m, (1, 4), (2, 3))
+    advance(ring_m, (1, 2), (2, 1))
+    inverse[...] = jnp.zeros_like(inverse)
+    advance(ring_m, (1, 3), (2, 2))
+    advance(ring_m, (1, 4))
     start_sketched(1)
-    advance(ring_s, (0, 1))
-    inverse[...] = jnp.zeros_like(inverse)
+    advance(ring_m, (2, 3))
+    pieces_in()
+    advance(ring_s, (1, 1))
     advance(ring_m, (2, 4))
-    advance(ring_s, (0, 2), (1, 1))
     start_sketched(2)
-    pieces_done()
-    advance(ring_s, (0, 3), (1, 2), (2, 1))
 
     def start_joint(c):
-        joint[c, me] = make_joint(c)
+        joint[c][me] = make_joint(c)
         ring_j.stage(c, 0)
 
     def finish_joint(c):
         ring_j.stage(c, 4)
         project(c)
 
+    def gram(c):
+        w, at0 = WIDTHS[c], starts[c]
+        sk_t[at(c), :] = sk[c][...].reshape(total, w).astype(f32).T.astype(bf16)
+        for b in range(c + 1):
+            xcol[at(b), at(c)] = dot(sk_t[at(b), :], sk[c][...].reshape(total, w), 1, 0)
+
     M, S, J = (lambda c, k, r=r: (r.stage, c, k) for r in (ring_m, ring_s, ring_j))
     even = {
-        0: [S(0, 4), S(1, 3), S(2, 2)],
-        1: [S(2, 4), J(0, 1)],
-        2: [J(0, 3), J(1, 1), (start_joint, 2)],
-        3: [J(1, 3), J(2, 2)],
-        4: [(finish_joint, 2)],
+        0: [(ring_s.direct_done, 0), (gram, 0)],
+        1: [S(1, 4), (gram, 1), S(2, 3), (pieces_done,)],
+        2: [J(0, 1), (start_joint, 2)],
+        3: [(gram, 2), J(0, 3), J(2, 1)],
+        4: [J(2, 2)],
+        5: [(finish_joint, 1)],
     }
     odd = {
-        0: [S(1, 4), S(2, 3), (start_joint, 0)],
-        1: [(start_joint, 1), J(0, 2)],
-        2: [(finish_joint, 0), J(1, 2), J(2, 1)],
-        3: [(finish_joint, 1), J(2, 3)],
+        0: [S(1, 3), S(2, 2)],
+        1: [S(2, 4), (start_joint, 0), (start_joint, 1)],
+        2: [J(0, 2), J(1, 1)],
+        3: [(finish_joint, 0), J(1, 2)],
+        4: [J(1, 3), J(2, 3)],
+        5: [(finish_joint, 2)],
     }
+    first = {0: [S(1, 2), S(2, 1)]}
 
     def run(c, table):
         for cc, todo in table.items():
@@ -352,68 +411,55 @@
 
     eye = lax.broadcasted_iota(jnp.int32, (B, B), 0) == lax.broadcasted_iota(jnp.int32, (B, B), 1)
 
-    blocks = chunks * (W // B)
+    blocks = sum(WIDTHS) // B
 
     def step(c, carry):
         here = pl.multiple_of(c * B, B)
-        ch = c // 2
-        off = pl.multiple_of((c % 2) * B, B)
         run(c, even)
-
-        @pl.when(c % 2 == 0)
-        def _():
-            sk_t[pl.ds(here, W), :] = sk[ch].reshape(total, W).astype(f32).T.astype(bf16)
-
-            def gram(i, cc):
-                ii = pl.multiple_of(i * W, W)
-                xcol[pl.ds(ii, W), :] = dot(sk_t[pl.ds(ii, W), :], sk[ch].reshape(total, W), 1, 0)
-                return cc
-
-            lax.fori_loop(0, ch + 1, gram, 0)
-
         for cc in range(1, blocks):
 
             @pl.when(c == cc)
-            def _(k=cc * B, mine=slice((cc % 2) * B, (cc % 2 + 1) * B)):
-                x = dot(inverse[0:k, 0:k], xcol[0:k, mine], 1, 0, precision=HIGH)
+            def _(k=cc * B, mine=slice(cc * B, (cc + 1) * B)):
+                x = dot3(inverse[0:k, 0:k], xcol[0:k, mine])
                 xt = x.T
-                xcol[k : k + B, mine] = xcol[k : k + B, mine] - dot(xt, x, 1, 0, precision=HIGH)
-                inverse[k : k + B, 0:k] = dot(xt, inverse[0:k, 0:k], 1, 0, precision=HIGH)
-
-        a = xcol[pl.ds(here, B), pl.ds(off, B)] + jnp.where(eye, 1.0 - colm[ch, :, pl.ds(off, B)], 0.0)
-        inv = pivot_inverse(a, {9: lambda: run(c, odd)})
+                xcol[k : k + B, mine] = xcol[k : k + B, mine] - dot3(xt, x)
+                inverse[k : k + B, 0:k] = dot3(xt, inverse[0:k, 0:k])
+
+        a = xcol[pl.ds(here, B), pl.ds(here, B)] + jnp.where(eye, 1.0 - colm[:, pl.ds(here, B)], 0.0)
+        inv = pivot_inverse(a, {2: lambda: run(c, first), 9: lambda: run(c, odd)})
         for cc in range(1, blocks):
 
             @pl.when(c == cc)
             def _(k=cc * B):
-                inverse[k : k + B, 0:k] = -dot(inv, inverse[k : k + B, 0:k], 1, 0, precision=HIGH)
+                inverse[k : k + B, 0:k] = -dot3(inv, inverse[k : k + B, 0:k])
 
         inverse[pl.ds(here, B), pl.ds(here, B)] = inv
         return carry
 
     lax.fori_loop(0, blocks, step, 0)
-    for c in range(chunks):
-        own_out[:, c * W : (c + 1) * W] = sk[c, me]
-
-    def drain(c, carry):
+    for c in range(len(WIDTHS)):
+        own_out[:, at(c)] = sk[c][me]
+    ring_m.direct_drain(0)
+    ring_s.direct_drain(0)
+    ring_j.drain(0)
+    for c in range(1, len(WIDTHS)):
         ring_m.drain(c)
         ring_s.drain(c)
         ring_j.drain(c)
-        return carry
-
-    lax.fori_loop(0, chunks, drain, 0)
     for copy in started:
         copy.wait_send()
 
 
-def bond(right, left, gates, sketch, rowm, colm):
+def bond(right, left, diag, hop, sketch, live_rows, kept):
     bf16, f32 = jnp.bfloat16, jnp.float32
     rows, middle = left.shape
     depth, columns = right.shape
     width = sketch.shape[1]
-    chunks = width // W
+    chunks = len(WIDTHS)
     cols_here = columns // BLKS
     vmem = pl.BlockSpec(memory_space=pltpu.VMEM)
+    smem = pl.BlockSpec(memory_space=pltpu.SMEM)
+    anyw = pl.BlockSpec(memory_space=pl.ANY)
     dma = pltpu.SemaphoreType.DMA
     return pl.pallas_call(
         bond_kernel,
@@ -422,23 +468,33 @@
             jax.ShapeDtypeStruct((cols_here, width), f32),
             jax.ShapeDtypeStruct((rows, width), bf16),
         ),
-        in_specs=[vmem, vmem, vmem, pl.BlockSpec(memory_space=pl.ANY), vmem, vmem],
+        in_specs=[anyw, anyw, anyw, anyw, anyw, smem, smem],
         out_specs=(vmem, vmem, vmem),
         scratch_shapes=[
+            pltpu.VMEM((depth, columns), bf16),
+            pltpu.VMEM((rows, middle), bf16),
+            pltpu.VMEM((1, columns), f32),
+            pltpu.VMEM((3, columns), f32),
+            pltpu.VMEM((rows, 1), f32),
+            pltpu.VMEM((1, width), f32),
             pltpu.VMEM((columns, width), bf16),
             pltpu.VMEM((3 * depth, columns), bf16),
-            pltpu.VMEM((chunks, BLKS, 3 * depth, W), bf16),
-            pltpu.VMEM((chunks, BLKS, rows, W), bf16),
+            *(pltpu.VMEM((BLKS, 3 * depth, w), bf16) for w in WIDTHS),
+            *(pltpu.VMEM((BLKS, rows, w), bf16) for w in WIDTHS),
             pltpu.VMEM((width, rows * BLKS), bf16),
-            pltpu.VMEM((chunks, BLKS, 3 * depth, W), bf16),
+            *(pltpu.VMEM((BLKS, 3 * depth, w), bf16) for w in WIDTHS),
             pltpu.VMEM((2, depth, columns), bf16),
             pltpu.VMEM((2, rows, middle), bf16),
-            pltpu.VMEM((BLKS, 2 * depth, rows), bf16),
-            pltpu.VMEM((3, BLKS, 2 * depth, rows), bf16),
+            pltpu.VMEM((BLKS, depth, cols_here + rows), bf16),
+            pltpu.VMEM((3, BLKS, depth, cols_here + rows), bf16),
             pltpu.VMEM((BLKS, 3, cols_here), f32),
             pltpu.VMEM((3 * depth, rows * BLKS), bf16),
             pltpu.VMEM((3, cols_here, middle), bf16),
-            pltpu.VMEM((width, W), f32),
+            pltpu.VMEM((width, width), f32),
+            dma(()),
+            dma(()),
+            dma(()),
+            dma(()),
             dma(()),
             dma(()),
             dma((4,)),
@@ -455,32 +511,21 @@
             dma((2,)),
         ],
         compiler_params=pltpu.CompilerParams(
-            collective_id=0, has_side_effects=True, vmem_limit_bytes=50 * 2**20
+            collective_id=0, has_side_effects=True, vmem_limit_bytes=60 * 2**20
         ),
-    )(right, left, gates, sketch, rowm, colm)
-
-
-def dot32(a, b, dims, **kw):
-    return lax.dot_general(a, b, (dims, ((), ())), preferred_element_type=jnp.float32, **kw)
+    )(right, left, diag, hop, sketch, live_rows, kept)
 
 
 def body(left_tensor, right_tensor, diag_gate, hop_gate, sketch, sector_rows, kept):
     f32 = jnp.float32
-    left, right, diag, hop = left_tensor[0], right_tensor[0], diag_gate[0], hop_gate[0]
-    rows_here, middle = left.shape
-    width = sketch.shape[1]
-    total = rows_here * lax.axis_size("blk")
-    g, me = lax.axis_index("grp"), lax.axis_index("blk")
-    hop_low = jnp.where(g > 0, hop, 0.0)
-    hop_high = jnp.where(g < lax.axis_size("grp") - 1, hop, 0.0)
-    gates = jnp.stack([diag, hop_low, hop_high])
-    row_index = me * rows_here + jnp.arange(rows_here, dtype=jnp.int32)
-    rowm = (row_index[:, None] < sector_rows[0]).astype(f32)
-    colm = (jnp.arange(width, dtype=jnp.int32).reshape(-1, 1, W) < kept[0]).astype(f32)
-    inverse, projected, sketched = bond(right, left, gates, sketch, rowm, colm)
-    scale = math.sqrt(total)
-    left_out = dot32(sketched.astype(f32), inverse, ((1,), (1,)), precision=HIGH) * scale
-    right_out = dot32(projected, inverse, ((1,), (1,)), precision=HIGH) / scale
+    inverse, projected, sketched = bond(
+        right_tensor[0], left_tensor[0], diag_gate, hop_gate, sketch, sector_rows, kept
+    )
+    scale = math.sqrt(left_tensor.shape[1] * lax.axis_size("blk"))
+    precise = dict(preferred_element_type=f32, precision=lax.Precision.HIGH)
+    solve = (((1,), (1,)), ((), ()))
+    left_out = lax.dot_general(sketched.astype(f32), inverse, solve, **precise) * scale
+    right_out = lax.dot_general(projected, inverse, solve, **precise) / scale
     return (left_out[None], right_out[:, None, :])
 
 

time: 134 us -> 123 us (0.918)
  Pallas kernels: 122 us -> 115 us
  local copies, waits for them, and re-layouts: 3.34 us -> 1.43 us
  other arithmetic: 1.5 us -> 0 us
    pallas_call x1, Pallas kernels: 122 us -> 115 us  [bond(): pl.pallas_call(bond_kernel, out_shape=(jax.ShapeDtypeStruct((width, width...]
    unnamed x5, local copies, waits for them, and re-layouts: 3.34 us -> 1.43 us
where the time goes in v4:
time: 123 us
  Pallas kernels  115 us (93%)
  matrix products  5.1 us (4%)
  between operations  1.96 us (2%)
  local copies, waits for them, and re-layouts  1.43 us (1%)
    pallas_call x1, Pallas kernels, bond(): pl.pallas_call(bond_kernel, out_shape=(jax.ShapeDtypeStruct((width, width...  115 us
    dot_general x1, matrix products, body(): right_out = lax.dot_general(projected, inverse, solve, **precise) / scale  3.35 us

profile of v4, /device:TPU:0, one launch (start us, length us, event | category | flops | bytes accessed | tf_op | source)
XLA Modules:
  0.0 123.1 jit_solution(12340020282210980672)
XLA Ops:
  1.9 114.6 %shard_map.86 = (f32[768,768]{1,0:T(8,128)}, f32[192,768]{1,0:T(8,128)}, bf16[192,768]{1,0:T(8,128)(2,1)}) custom-call(bf16[48,3072]{1,0:T(8,128)(2,1)} %bitcast.10, bf16[192,768]{1,0:T(8,128)(2,1)} %bitcast.11, f32[1,3072]{1,0:T(1,128)} %diag_hbm.1, f32[1,3072]{1,0:T(1,128)} %hop_hbm.1, bf16[3072,768]{1,0:T(8,128)(2,1)} %sketch_hbm.1, ...), custom_call_target="tpu_custom_call" | custom-call | tf_op jit(solution)/shard_map/pallas_call | solution.py:464
  116.5 0.0 copy-start
  116.5 0.0 copy-start.1
  116.5 3.3 %fusion = f32[192,1,768]{2,0,1:T(8,128)S(1)} fusion(f32[192,768]{1,0:T(8,128)} %get-tuple-element.7, f32[768,768]{1,0:T(8,128)} %get-tuple-element.6), kind=kOutput, calls=%fused_computation.1 | convolution fusion | flops 679624704 | bytes 3538944 | tf_op jit(solution)/shard_map/dot_general | solution.py:528
  119.9 1.4 %copy.9 = f32[192,1,768]{2,1,0:T(1,128)} copy(f32[192,1,768]{2,0,1:T(8,128)S(1)} %fusion) | data formatting | bytes 1179648
  121.3 0.0 copy-done
  121.3 0.0 copy-done.1
  121.3 1.8 %fusion.1 = f32[1,192,768]{2,1,0:T(8,128)} fusion(bf16[192,768]{1,0:T(8,128)(2,1)S(1)} %copy-done.1, f32[768,768]{1,0:T(8,128)S(1)} %copy-done), kind=kOutput, calls=%fused_computation.3 | convolution fusion | flops 679624704 | bytes 3244032 | tf_op jit(solution)/shard_map/dot_general | solution.py:527
Async XLA Ops:
  116.5 4.8 %copy-start = (f32[768,768]{1,0:T(8,128)S(1)}, f32[768,768]{1,0:T(8,128)}, u32[]{:S(2)}) copy-start(f32[768,768]{1,0:T(8,128)} %get-tuple-element.6) | copy-start | bytes 7077892
  116.5 4.8 %copy-start.1 = (bf16[192,768]{1,0:T(8,128)(2,1)S(1)}, bf16[192,768]{1,0:T(8,128)(2,1)}, u32[]{:S(2)}) copy-start(bf16[192,768]{1,0:T(8,128)(2,1)} %get-tuple-element.5) | copy-start | bytes 884740

commit v5 on v4

--- a/solution.py
+++ b/solution.py
@@ -9,7 +9,7 @@
 
 HIGH = lax.Precision.HIGHEST
 B = 128
-WIDTHS = (B, 2 * B, 3 * B)
+WIDTHS = (B, 3 * B, 2 * B)
 SIDE = 4
 BLKS = SIDE * SIDE
 MESH = pl.DeviceIdType.MESH
@@ -358,15 +358,16 @@
         x_wait(left_n.at[slot], 2 + slot)
     start_sketched(0)
     advance(ring_m, (1, 2), (2, 1))
+    pieces_in()
+    advance(ring_m, (1, 3), (2, 2), (1, 4))
+    start_sketched(1)
     inverse[...] = jnp.zeros_like(inverse)
-    advance(ring_m, (1, 3), (2, 2))
-    advance(ring_m, (1, 4))
-    start_sketched(1)
     advance(ring_m, (2, 3))
-    pieces_in()
     advance(ring_s, (1, 1))
+    pieces_done()
     advance(ring_m, (2, 4))
     start_sketched(2)
+    advance(ring_s, (1, 2))
 
     def start_joint(c):
         joint[c][me] = make_joint(c)
@@ -383,23 +384,32 @@
             xcol[at(b), at(c)] = dot(sk_t[at(b), :], sk[c][...].reshape(total, w), 1, 0)
 
     M, S, J = (lambda c, k, r=r: (r.stage, c, k) for r in (ring_m, ring_s, ring_j))
+    def sent():
+        for copy in started:
+            copy.wait_send()
+
+    def own():
+        for c in range(len(WIDTHS)):
+            own_out[:, at(c)] = sk[c][me]
+
     even = {
         0: [(ring_s.direct_done, 0), (gram, 0)],
-        1: [S(1, 4), (gram, 1), S(2, 3), (pieces_done,)],
-        2: [J(0, 1), (start_joint, 2)],
-        3: [(gram, 2), J(0, 3), J(2, 1)],
-        4: [J(2, 2)],
-        5: [(finish_joint, 1)],
+        1: [S(1, 4), (gram, 1), S(2, 3), (start_joint, 0)],
+        2: [J(0, 1), (start_joint, 2), (ring_m.direct_drain, 0), (sent,)],
+        3: [J(0, 3), J(2, 1), (ring_m.drain, 1)],
+        4: [(gram, 2), J(1, 3), J(2, 2), (ring_s.direct_drain, 0)],
+        5: [(finish_joint, 1), (ring_j.drain, 0), (own,)],
     }
     odd = {
-        0: [S(1, 3), S(2, 2)],
-        1: [S(2, 4), (start_joint, 0), (start_joint, 1)],
-        2: [J(0, 2), J(1, 1)],
-        3: [(finish_joint, 0), J(1, 2)],
-        4: [J(1, 3), J(2, 3)],
-        5: [(finish_joint, 2)],
+        0: [S(1, 3)],
+        1: [S(2, 4), (start_joint, 1)],
+        2: [J(0, 2), J(1, 1), (ring_m.drain, 2)],
+        3: [(finish_joint, 0), J(1, 2), (ring_s.drain, 1)],
+        4: [J(2, 3), (ring_s.drain, 2)],
+        5: [(ring_j.drain, 1), (finish_joint, 2)],
     }
-    first = {0: [S(1, 2), S(2, 1)]}
+    first = {0: [S(2, 1)]}
+    third = {0: [S(2, 2)]}
 
     def run(c, table):
         for cc, todo in table.items():
@@ -426,7 +436,7 @@
                 inverse[k : k + B, 0:k] = dot3(xt, inverse[0:k, 0:k])
 
         a = xcol[pl.ds(here, B), pl.ds(here, B)] + jnp.where(eye, 1.0 - colm[:, pl.ds(here, B)], 0.0)
-        inv = pivot_inverse(a, {2: lambda: run(c, first), 9: lambda: run(c, odd)})
+        inv = pivot_inverse(a, {3: lambda: run(c, first), 8: lambda: run(c, odd), 13: lambda: run(c, third)})
         for cc in range(1, blocks):
 
             @pl.when(c == cc)
@@ -437,17 +447,7 @@
         return carry
 
     lax.fori_loop(0, blocks, step, 0)
-    for c in range(len(WIDTHS)):
-        own_out[:, at(c)] = sk[c][me]
-    ring_m.direct_drain(0)
-    ring_s.direct_drain(0)
-    ring_j.drain(0)
-    for c in range(1, len(WIDTHS)):
-        ring_m.drain(c)
-        ring_s.drain(c)
-        ring_j.drain(c)
-    for copy in started:
-        copy.wait_send()
+    ring_j.drain(2)
 
 
 def bond(right, left, diag, hop, sketch, live_rows, kept):

time: 123 us -> 121 us (0.984)
  Pallas kernels: 115 us -> 112 us
    pallas_call x1, Pallas kernels: 115 us -> 112 us  [bond(): pl.pallas_call(bond_kernel, out_shape=(jax.ShapeDtypeStruct((width, width...]
where the time goes in v5:
time: 121 us
  Pallas kernels  112 us (93%)
  matrix products  5.1 us (4%)
  between operations  1.96 us (2%)
  local copies, waits for them, and re-layouts  1.43 us (1%)
    pallas_call x1, Pallas kernels, bond(): pl.pallas_call(bond_kernel, out_shape=(jax.ShapeDtypeStruct((width, width...  112 us
    dot_general x1, matrix products, body(): right_out = lax.dot_general(projected, inverse, solve, **precise) / scale  3.35 us

profile of v5, /device:TPU:0, one launch (start us, length us, event | category | flops | bytes accessed | tf_op | source)
XLA Modules:
  0.0 120.7 jit_solution(16164167333374454379)
XLA Ops:
  1.9 112.2 %shard_map.86 = (f32[768,768]{1,0:T(8,128)}, f32[192,768]{1,0:T(8,128)}, bf16[192,768]{1,0:T(8,128)(2,1)}) custom-call(bf16[48,3072]{1,0:T(8,128)(2,1)} %bitcast.10, bf16[192,768]{1,0:T(8,128)(2,1)} %bitcast.11, f32[1,3072]{1,0:T(1,128)} %diag_hbm.1, f32[1,3072]{1,0:T(1,128)} %hop_hbm.1, bf16[3072,768]{1,0:T(8,128)(2,1)} %sketch_hbm.1, ...), custom_call_target="tpu_custom_call" | custom-call | tf_op jit(solution)/shard_map/pallas_call | solution.py:464
  114.2 0.0 copy-start
  114.2 0.0 copy-start.1
  114.2 3.3 %fusion = f32[192,1,768]{2,0,1:T(8,128)S(1)} fusion(f32[192,768]{1,0:T(8,128)} %get-tuple-element.7, f32[768,768]{1,0:T(8,128)} %get-tuple-element.6), kind=kOutput, calls=%fused_computation.1 | convolution fusion | flops 679624704 | bytes 3538944 | tf_op jit(solution)/shard_map/dot_general | solution.py:528
  117.5 1.4 %copy.9 = f32[192,1,768]{2,1,0:T(1,128)} copy(f32[192,1,768]{2,0,1:T(8,128)S(1)} %fusion) | data formatting | bytes 1179648
  118.9 0.0 copy-done
  118.9 0.0 copy-done.1
  119.0 1.8 %fusion.1 = f32[1,192,768]{2,1,0:T(8,128)} fusion(bf16[192,768]{1,0:T(8,128)(2,1)S(1)} %copy-done.1, f32[768,768]{1,0:T(8,128)S(1)} %copy-done), kind=kOutput, calls=%fused_computation.3 | convolution fusion | flops 679624704 | bytes 3244032 | tf_op jit(solution)/shard_map/dot_general | solution.py:527
Async XLA Ops:
  114.2 4.8 %copy-start = (f32[768,768]{1,0:T(8,128)S(1)}, f32[768,768]{1,0:T(8,128)}, u32[]{:S(2)}) copy-start(f32[768,768]{1,0:T(8,128)} %get-tuple-element.6) | copy-start | bytes 7077892
  114.2 4.8 %copy-start.1 = (bf16[192,768]{1,0:T(8,128)(2,1)S(1)}, bf16[192,768]{1,0:T(8,128)(2,1)}, u32[]{:S(2)}) copy-start(bf16[192,768]{1,0:T(8,128)(2,1)} %get-tuple-element.5) | copy-start | bytes 884740

commit v6 on v5

--- a/solution.py
+++ b/solution.py
@@ -394,17 +394,17 @@
 
     even = {
         0: [(ring_s.direct_done, 0), (gram, 0)],
-        1: [S(1, 4), (gram, 1), S(2, 3), (start_joint, 0)],
-        2: [J(0, 1), (start_joint, 2), (ring_m.direct_drain, 0), (sent,)],
-        3: [J(0, 3), J(2, 1), (ring_m.drain, 1)],
+        1: [S(1, 4), (gram, 1), S(2, 3)],
+        2: [(start_joint, 2), (ring_m.direct_drain, 0), (sent,)],
+        3: [J(0, 2), J(2, 1), (ring_m.drain, 1)],
         4: [(gram, 2), J(1, 3), J(2, 2), (ring_s.direct_drain, 0)],
-        5: [(finish_joint, 1), (ring_j.drain, 0), (own,)],
+        5: [(finish_joint, 0), (finish_joint, 1), (ring_j.drain, 0), (own,)],
     }
     odd = {
         0: [S(1, 3)],
-        1: [S(2, 4), (start_joint, 1)],
-        2: [J(0, 2), J(1, 1), (ring_m.drain, 2)],
-        3: [(finish_joint, 0), J(1, 2), (ring_s.drain, 1)],
+        1: [S(2, 4), (start_joint, 1), (start_joint, 0)],
+        2: [J(1, 1), J(0, 1), (ring_m.drain, 2)],
+        3: [J(1, 2), J(0, 3), (ring_s.drain, 1)],
         4: [J(2, 3), (ring_s.drain, 2)],
         5: [(ring_j.drain, 1), (finish_joint, 2)],
     }

time: 121 us -> 125 us (1.033)
  Pallas kernels: 112 us -> 116 us
    pallas_call x1, Pallas kernels: 112 us -> 116 us  [bond(): pl.pallas_call(bond_kernel, out_shape=(jax.ShapeDtypeStruct((width, width...]
where the time goes in v6:
time: 125 us
  Pallas kernels  116 us (93%)
  matrix products  5.1 us (4%)
  between operations  1.96 us (2%)
  local copies, waits for them, and re-layouts  1.43 us (1%)
    pallas_call x1, Pallas kernels, bond(): pl.pallas_call(bond_kernel, out_shape=(jax.ShapeDtypeStruct((width, width...  116 us
    dot_general x1, matrix products, body(): right_out = lax.dot_general(projected, inverse, solve, **precise) / scale  3.35 us

profile of v6, /device:TPU:0, one launch (start us, length us, event | category | flops | bytes accessed | tf_op | source)
XLA Modules:
  0.0 124.7 jit_solution(2497373637619480600)
XLA Ops:
  1.9 116.2 %shard_map.86 = (f32[768,768]{1,0:T(8,128)}, f32[192,768]{1,0:T(8,128)}, bf16[192,768]{1,0:T(8,128)(2,1)}) custom-call(bf16[48,3072]{1,0:T(8,128)(2,1)} %bitcast.10, bf16[192,768]{1,0:T(8,128)(2,1)} %bitcast.11, f32[1,3072]{1,0:T(1,128)} %diag_hbm.1, f32[1,3072]{1,0:T(1,128)} %hop_hbm.1, bf16[3072,768]{1,0:T(8,128)(2,1)} %sketch_hbm.1, ...), custom_call_target="tpu_custom_call" | custom-call | tf_op jit(solution)/shard_map/pallas_call | solution.py:464
  118.1 0.0 copy-start
  118.1 0.0 copy-start.1
  118.2 3.3 %fusion = f32[192,1,768]{2,0,1:T(8,128)S(1)} fusion(f32[192,768]{1,0:T(8,128)} %get-tuple-element.7, f32[768,768]{1,0:T(8,128)} %get-tuple-element.6), kind=kOutput, calls=%fused_computation.1 | convolution fusion | flops 679624704 | bytes 3538944 | tf_op jit(solution)/shard_map/dot_general | solution.py:528
  121.5 1.4 %copy.9 = f32[192,1,768]{2,1,0:T(1,128)} copy(f32[192,1,768]{2,0,1:T(8,128)S(1)} %fusion) | data formatting | bytes 1179648
  122.9 0.0 copy-done
  122.9 0.0 copy-done.1
  122.9 1.8 %fusion.1 = f32[1,192,768]{2,1,0:T(8,128)} fusion(bf16[192,768]{1,0:T(8,128)(2,1)S(1)} %copy-done.1, f32[768,768]{1,0:T(8,128)S(1)} %copy-done), kind=kOutput, calls=%fused_computation.3 | convolution fusion | flops 679624704 | bytes 3244032 | tf_op jit(solution)/shard_map/dot_general | solution.py:527
Async XLA Ops:
  118.1 4.8 %copy-start = (f32[768,768]{1,0:T(8,128)S(1)}, f32[768,768]{1,0:T(8,128)}, u32[]{:S(2)}) copy-start(f32[768,768]{1,0:T(8,128)} %get-tuple-element.6) | copy-start | bytes 7077892
  118.1 4.8 %copy-start.1 = (bf16[192,768]{1,0:T(8,128)(2,1)S(1)}, bf16[192,768]{1,0:T(8,128)(2,1)}, u32[]{:S(2)}) copy-start(bf16[192,768]{1,0:T(8,128)(2,1)} %get-tuple-element.5) | copy-start | bytes 884740
